TPU v7x, 256 devices: a whole 4x4x8 slice. The times are simulated.
256 devices in a mesh: fsdp: 8 (over y_hi, x), context: 32 (over z, y_lo, core).
Axes of the slice: x: 4, y: 4 (y_hi: 2, y_lo: 2; y = y_hi * 2 + y_lo), z: 8, core: 2. Of those that a mesh axis runs over, the one named last changes fastest.
Arguments:
- inputs: bfloat16 [8, 4096, 8192], P('fsdp', 'context'), may hold values from -6 to 6
- queries: bfloat16 [8, 4096, 4096], P('fsdp', 'context'), may hold values from -70 to 70, as said below
- values: bfloat16 [8, 4096, 512], P('fsdp', 'context'), may hold values from -6 to 6
- output_gradient: bfloat16 [8, 4096, 4096], P('fsdp', 'context'), may hold values from -6 to 6
- key_base_weight: bfloat16 [8192, 512], P('fsdp'), may hold values from -0.0625 to 0.0625
- adapter_down: bfloat16 [8192, 64], P('fsdp'), may hold values from -0.0625 to 0.0625
- adapter_up: bfloat16 [64, 512], P(None, 'fsdp'), may hold values from -0.75 to 0.75
- span_slot_index: int32 [8, 64], P('fsdp'), may hold values from 0 to 63, each once within a row
- segment_document: int32 [8, 4096], P('fsdp'), may hold values from 0 to 31, never falling along the last dimension, each value on 1 to 1024 neighbouring positions
Outputs:
- query_grad: bfloat16 [8, 4096, 4096], P('fsdp', 'context')
- value_grad: bfloat16 [8, 4096, 512], P('fsdp', 'context')
- input_gradient: bfloat16 [8, 4096, 8192], P('fsdp', 'context')
- down_grad: float32 [8192, 64], P('fsdp')
- up_grad: float32 [64, 512], P(None, 'fsdp')
Inputs may be any that keep to these rules, and one draw needn't show every extreme that they name: `queries`: in the shown draw standard normal clipped to 6; rows may carry scales up to fortyfold.
All inputs are finite; a program needn't handle non-finite values.
Results may differ from a plain program's by a relative error of at most 0.04.
Values may be sent and summed in bfloat16 or wider, within the bound.
A program may use at most 256 MiB of HBM per device.

v0:
```python
import math

import jax
import jax.numpy as jnp
from jax import lax
from jax.sharding import PartitionSpec as P

QUERY_HEADS = 32
KEY_VALUE_HEADS = 4
HEAD_SIZE = 128


ADAPTER_SCALE = 0.5
NEGATIVE_FILL = -1e30


def body(
    inputs,
    queries,
    values,
    output_gradient,
    key_base_weight,
    adapter_down,
    adapter_up,
    span_slot_index,
    segment_document,
):
    tokens = inputs.shape[1]
    span_length = tokens // 2
    query_groups = QUERY_HEADS // KEY_VALUE_HEADS
    kv_width = values.shape[2]
    inv_root = 1.0 / math.sqrt(HEAD_SIZE)
    full_key, complete_down, complete_up = (
        lax.all_gather(key_base_weight, "fsdp", axis=0, tiled=True),
        lax.all_gather(adapter_down, "fsdp", axis=0, tiled=True),
        lax.all_gather(adapter_up, "fsdp", axis=1, tiled=True),
    )
    rows_in = inputs[0]
    reduced_rank_input = jnp.dot(rows_in, complete_down, preferred_element_type=jnp.float32).astype(
        jnp.bfloat16
    )
    key_matrix = (
        jnp.dot(rows_in, full_key, preferred_element_type=jnp.float32)
        + ADAPTER_SCALE
        * jnp.dot(reduced_rank_input, complete_up, preferred_element_type=jnp.float32)
    ).astype(jnp.bfloat16)
    span_listing = span_slot_index[0]
    document_index = segment_document[0]
    length = document_index.shape[0]
    own_index = lax.axis_index("context")
    local_rows = jnp.arange(tokens, dtype=jnp.int32)
    own_pos = (
        span_listing[own_index * 2 + local_rows // span_length] * span_length
        + local_rows % span_length
    )
    query_pos = own_pos.reshape(2, span_length)
    query_doc = document_index[own_pos].reshape(2, span_length)
    query_head_split = queries[0].reshape(2, span_length, KEY_VALUE_HEADS, query_groups, HEAD_SIZE)
    gradient_heads = output_gradient[0].reshape(
        2, span_length, KEY_VALUE_HEADS, query_groups, HEAD_SIZE
    )

    def piece_info(sequence_portion, start):
        key_total_count = sequence_portion[0].shape[0]
        row_ids = start + jnp.arange(key_total_count, dtype=jnp.int32)
        key_pos = span_listing[row_ids // span_length] * span_length + row_ids % span_length
        key_doc = document_index[key_pos]
        key_head_split = sequence_portion[0].reshape(key_total_count, KEY_VALUE_HEADS, HEAD_SIZE)
        value_head_split = sequence_portion[1].reshape(key_total_count, KEY_VALUE_HEADS, HEAD_SIZE)
        masks = [
            (query_doc[h][:, None] == key_doc[None, :])
            & (key_pos[None, :] <= query_pos[h][:, None])
            for h in range(2)
        ]
        return (masks, key_head_split, value_head_split)

    def scores_of(half_index, allowed, key_head_split, value_head_split):
        products = (
            jnp.einsum(
                "qhgd,khd->hgqk",
                query_head_split[half_index],
                key_head_split,
                preferred_element_type=jnp.float32,
            )
            * inv_root
        )
        grad_prob = jnp.einsum(
            "qhgd,khd->hgqk",
            gradient_heads[half_index],
            value_head_split,
            preferred_element_type=jnp.float32,
        )
        return (jnp.where(allowed, products, NEGATIVE_FILL), grad_prob)

    def keep_state(carried):
        return carried[0]

    def first_pass(carry, sequence_portion, start):
        masks, key_head_split, value_head_split = piece_info(sequence_portion, start)
        updated = []
        for half_index in range(2):

            def first_update(carried, half_index=half_index):
                (peak_now, normalizer, weighted), allowed = carried
                scores, grad_prob = scores_of(half_index, allowed, key_head_split, value_head_split)
                new_peak = jnp.maximum(peak_now, jnp.max(scores, axis=-1))
                weights = jnp.where(allowed, jnp.exp(scores - new_peak[..., None]), 0.0)
                shrink = jnp.exp(peak_now - new_peak)
                return (
                    new_peak,
                    normalizer * shrink + jnp.sum(weights, axis=-1),
                    weighted * shrink + jnp.sum(weights * grad_prob, axis=-1),
                )

            state = (carry[0][half_index], carry[1][half_index], carry[2][half_index])
            updated.append(
                lax.cond(
                    jnp.any(masks[half_index]), first_update, keep_state, (state, masks[half_index])
                )
            )
        return tuple((jnp.stack([updated[0][k], updated[1][k]]) for k in range(3)))

    def second_pass(carry, sequence_portion, start):
        masks, key_head_split, value_head_split = piece_info(sequence_portion, start)
        key_total_count = key_head_split.shape[0]
        query_acc, key_sums = carry
        key_terms = jnp.zeros((key_total_count, 2 * kv_width), jnp.float32)
        query_parts = []
        for half_index in range(2):

            def second_update(carried, half_index=half_index):
                (query_half, terms_now), allowed = carried
                scores, grad_prob = scores_of(half_index, allowed, key_head_split, value_head_split)
                probability = jnp.where(
                    allowed, jnp.exp(scores - log_norm[half_index][..., None]), 0.0
                )
                prob_low = probability.astype(jnp.bfloat16)
                dscore = (
                    probability * (grad_prob - row_terms[half_index][..., None]) * inv_root
                ).astype(jnp.bfloat16)
                query_half = query_half + jnp.einsum(
                    "hgqk,khd->qhgd", dscore, key_head_split, preferred_element_type=jnp.float32
                )
                key_part = jnp.einsum(
                    "hgqk,qhgd->khd",
                    dscore,
                    query_head_split[half_index],
                    preferred_element_type=jnp.float32,
                )
                value_part = jnp.einsum(
                    "hgqk,qhgd->khd",
                    prob_low,
                    gradient_heads[half_index],
                    preferred_element_type=jnp.float32,
                )
                both = jnp.concatenate(
                    [
                        key_part.reshape(key_total_count, kv_width),
                        value_part.reshape(key_total_count, kv_width),
                    ],
                    axis=1,
                )
                return (query_half, terms_now + both)

            query_half, key_terms = lax.cond(
                jnp.any(masks[half_index]),
                second_update,
                keep_state,
                ((query_acc[half_index], key_terms), masks[half_index]),
            )
            query_parts.append(query_half)
        previous = lax.dynamic_slice_in_dim(key_sums, start, key_total_count, 0)
        key_sums = lax.dynamic_update_slice_in_dim(key_sums, previous + key_terms, start, 0)
        return (jnp.stack(query_parts), key_sums)

    zeroed_statistic = jnp.zeros((2, KEY_VALUE_HEADS, query_groups, span_length), jnp.float32)
    initial_forward = (
        jnp.full((2, KEY_VALUE_HEADS, query_groups, span_length), NEGATIVE_FILL, jnp.float32),
        zeroed_statistic,
        zeroed_statistic,
    )
    second_init = (
        jnp.zeros((2, span_length, KEY_VALUE_HEADS, query_groups, HEAD_SIZE), jnp.float32),
        jnp.zeros((length, 2 * kv_width), jnp.float32),
    )
    own_values = values[0]
    gathered = (
        lax.all_gather(key_matrix, "context", axis=0, tiled=True),
        lax.all_gather(own_values, "context", axis=0, tiled=True),
    )
    shard_count = length // tokens
    block_rows = tokens * max(1, shard_count // 16)
    block_keys = gathered[0].reshape(-1, block_rows, kv_width)
    block_values = gathered[1].reshape(-1, block_rows, kv_width)
    block_ids = jnp.arange(block_keys.shape[0], dtype=jnp.int32)

    def run_blocks(fold_fn, init):

        def block_step(carry, block_item):
            return (
                fold_fn(carry, (block_item[1], block_item[2]), block_item[0] * block_rows),
                None,
            )

        result, _ = lax.scan(block_step, init, (block_ids, block_keys, block_values))
        return result

    peaks, normalizers, weighted = run_blocks(first_pass, initial_forward)
    log_norm = peaks + jnp.log(normalizers)
    row_terms = weighted / normalizers
    query_acc, key_sums = run_blocks(second_pass, second_init)
    owned_sums = lax.psum_scatter(
        key_sums.astype(jnp.bfloat16), "context", scatter_dimension=0, tiled=True
    ).astype(jnp.float32)
    key_gradient = owned_sums[:, :kv_width].astype(jnp.bfloat16)
    value_grad = owned_sums[:, kv_width:].astype(jnp.bfloat16)
    query_grad = query_acc.reshape(tokens, QUERY_HEADS * HEAD_SIZE).astype(jnp.bfloat16)
    key_lifted = jnp.dot(key_gradient, complete_up.T, preferred_element_type=jnp.float32).astype(
        jnp.bfloat16
    )
    input_gradient = (
        jnp.dot(key_gradient, full_key.T, preferred_element_type=jnp.float32)
        + ADAPTER_SCALE * jnp.dot(key_lifted, complete_down.T, preferred_element_type=jnp.float32)
    ).astype(jnp.bfloat16)
    down_resident = ADAPTER_SCALE * jnp.einsum(
        "td,tr->dr", rows_in, key_lifted, preferred_element_type=jnp.float32
    )
    up_resident = ADAPTER_SCALE * jnp.einsum(
        "tr,tk->rk", reduced_rank_input, key_gradient, preferred_element_type=jnp.float32
    )
    summed = lax.psum((down_resident, up_resident), "context")
    down_share, up_share = (
        lax.psum_scatter(summed[0], "fsdp", scatter_dimension=0, tiled=True),
        lax.psum_scatter(summed[1], "fsdp", scatter_dimension=1, tiled=True),
    )
    return (query_grad[None], value_grad[None], input_gradient[None], down_share, up_share)


def solution(mesh):
    placed = (
        P("fsdp", "context", None),
        P("fsdp", "context", None),
        P("fsdp", "context", None),
        P("fsdp", "context", None),
        P("fsdp", None),
        P("fsdp", None),
        P(None, "fsdp"),
        P("fsdp", None),
        P("fsdp", None),
    )
    return jax.shard_map(
        body,
        mesh=mesh,
        in_specs=placed,
        out_specs=(
            P("fsdp", "context", None),
            P("fsdp", "context", None),
            P("fsdp", "context", None),
            P("fsdp", None),
            P(None, "fsdp"),
        ),
        check_vma=False,
    )
```

profile of v0, /device:TPU:1, one launch (start us, length us, event | category | flops | bytes accessed | tf_op | source)
XLA Modules:
  0.0 1711.3 jit_solution(15679124537329298174)
XLA Ops:
  10.2 29.3 %all_gather.17 = bf16[64,512]{0,1:T(8,128)(2,1)S(1)} all-gather(bf16[64,64]{0,1:T(8,128)(2,1)S(1)} %copy.58), channel_id=1, replica_groups=mesh['fsdp'=8,'context'=32] {'fsdp'}, dimensions={1}, use_global_device_ids=true | all-gather | bytes 73728 | tf_op jit(solution)/shard_map/all_gather | solution.py:36
  39.6 26.4 %all-gather.8.cloned.1.call-done = bf16[8192,64]{0,1:T(8,128)(2,1)} async-done(((bf16[1024,64]{0,1:T(8,128)(2,1)}), bf16[8192,64]{0,1:T(8,128)(2,1)}) %all-gather.8.cloned.1.call-update) | async-done | bytes 1048592 | tf_op jit(solution)/shard_map/all_gather | solution.py:35
  68.1 113.9 %all-gather.6.cloned.1.call-done = bf16[8192,512]{1,0:T(8,128)(2,1)} async-done(((bf16[1024,512]{1,0:T(8,128)(2,1)}), bf16[8192,512]{1,0:T(8,128)(2,1)}) %all-gather.6.cloned.1.call-update) | async-done | bytes 8388624 | tf_op jit(solution)/shard_map/all_gather | solution.py:34
  182.0 4.6 fusion.76
  192.6 56.9 %all-gather.12.cloned.1.call-done = bf16[1,4096,512]{2,1,0:T(8,128)(2,1)} async-done(((bf16[1,128,512]{2,1,0:T(8,128)(2,1)}), bf16[1,4096,512]{2,1,0:T(8,128)(2,1)}) %all-gather.12.cloned.1.call-update) | async-done | bytes 4194320 | tf_op jit(solution)/shard_map/all_gather | solution.py:189
  249.5 6.4 copy.64
  255.9 62.4 %all-gather.10.cloned.1.call-done = bf16[4096,512]{1,0:T(8,128)(2,1)} async-done(((bf16[128,512]{1,0:T(8,128)(2,1)}), bf16[4096,512]{1,0:T(8,128)(2,1)}) %all-gather.10.cloned.1.call-update) | async-done | bytes 4194320 | tf_op jit(solution)/shard_map/all_gather | solution.py:188
  318.3 6.4 copy.63
  324.7 256.6 %while.30 = (s32[]{:T(128)}, f32[2,4,8,64]{3,2,1,0:T(8,128)S(1)}, f32[2,4,8,64]{3,2,1,0:T(8,128)S(1)}, f32[2,4,8,64]{3,2,1,0:T(8,128)S(1)}, s32[2,64]{1,0:T(2,12...) while((s32[]{:T(128)}, f32[2,4,8,64]{3,2,1,0:T(8,128)S(1)}, ...), condition=%wide.region_13.14_spmd, body=%wide.region_0.13_spmd.sunk | while | flops 551721216 | bytes 17460676 | solution.py:205
  335.6 6.3 conditional.9
  342.4 6.3 conditional.8
  399.7 6.3 conditional.9
  418.9 6.3 conditional.9
  425.8 6.3 conditional.8
  444.3 6.3 conditional.9
  489.3 6.3 conditional.9
  522.0 6.3 conditional.8
  583.0 7.9 broadcast_in_dim.78.clone
  590.9 460.4 %while.31 = (s32[]{:T(128)}, f32[2,64,4,8,128]{4,1,3,2,0:T(8,128)}, f32[4096,1024]{1,0:T(8,128)}, s32[2,64]{1,0:T(2,128)S(1)}, s32[16]{0:T(128)S(1)}, /*index=5*...) while((s32[]{:T(128)}, f32[2,64,4,8,128]{4,1,3,2,0:T(8,128)}, ...), condition=%wide.region_21.22_spmd, body=%wide.region_14.21_spmd.sunk | while | flops 1353857280 | bytes 97210096 | solution.py:205
  604.6 2.8 slice_bitcast_fusion.30
  607.4 2.6 conditional.10
  611.0 5.8 conditional.11
  616.9 3.2 pad_maximum_fusion.12
  639.8 2.8 slice_bitcast_fusion.30
  643.7 3.2 pad_maximum_fusion.12
  666.7 2.8 slice_bitcast_fusion.30
  670.6 3.2 pad_maximum_fusion.12
  693.5 2.8 slice_bitcast_fusion.30
  697.5 3.2 pad_maximum_fusion.12
  720.4 2.8 slice_bitcast_fusion.30
  726.9 3.2 pad_maximum_fusion.12
  749.9 2.8 slice_bitcast_fusion.30
  756.3 5.8 conditional.11
  762.2 3.2 pad_maximum_fusion.12
  785.1 2.8 slice_bitcast_fusion.30
  791.6 3.2 pad_maximum_fusion.12
  814.5 2.8 slice_bitcast_fusion.30
  818.4 3.2 pad_maximum_fusion.12
  841.5 2.8 slice_bitcast_fusion.30
  845.4 3.2 pad_maximum_fusion.12
  868.4 2.8 slice_bitcast_fusion.30
  871.2 2.6 conditional.10
  874.9 3.2 pad_maximum_fusion.12
  897.8 2.8 slice_bitcast_fusion.30
  901.8 3.2 pad_maximum_fusion.12
  924.7 2.8 slice_bitcast_fusion.30
  928.6 5.8 conditional.11
  934.5 3.2 pad_maximum_fusion.12
  957.5 2.8 slice_bitcast_fusion.30
  961.4 3.2 pad_maximum_fusion.12
  984.3 2.8 slice_bitcast_fusion.30
  988.3 3.2 pad_maximum_fusion.12
  1011.2 2.8 slice_bitcast_fusion.30
  1015.1 3.2 pad_maximum_fusion.12
  1038.1 2.8 slice_bitcast_fusion.30
  1042.0 3.2 pad_maximum_fusion.12
  1051.3 9.1 convert_element_type.71
  1060.4 252.7 %reduce-scatter.6.cloned.1.call-done = bf16[128,1024]{1,0:T(8,128)(2,1)} async-done(((bf16[4096,1024]{1,0:T(8,128)(2,1)}), bf16[128,1024]{1,0:T(8,128)(2,1)}) %reduce-scatter.6.cloned.1.call-update) | async-done | bytes 262160 | tf_op jit(solution)/shard_map/reduce_scatter | solution.py:212
  1321.0 8.2 fusion.85
  1329.2 68.9 %reduce-scatter.8.cloned.1.call-done = f32[1024,64]{0,1:T(8,128)} async-done(((f32[8192,64]{0,1:T(8,128)}), f32[1024,64]{0,1:T(8,128)}) %reduce-scatter.8.cloned.1.call-update) | async-done | bytes 262160 | tf_op jit(solution)/shard_map/reduce_scatter | solution.py:233
  1398.2 4.3 fusion.71
  1403.1 73.5 %reduce-scatter.10.cloned.1.call-done = f32[64,64]{1,0:T(8,128)} async-done(((f32[512,64]{1,0:T(8,128)}), f32[64,64]{1,0:T(8,128)}) %reduce-scatter.10.cloned.1.call-update) | async-done | bytes 16400
  1477.5 103.6 %psum.17 = f32[64,64]{1,0:T(8,128)} all-reduce(f32[64,64]{1,0:T(8,128)S(1)} %copy.98), channel_id=1, replica_groups=mesh['fsdp'=8,'context'=32] {'context'}, use_global_device_ids=true, to_apply=%region_25.26 | all-reduce | flops 4096 | bytes 32768 | tf_op jit(solution)/shard_map/psum | solution.py:231
  1581.1 121.7 %all-reduce.2.cloned.1.call-done = f32[1024,64]{0,1:T(8,128)} async-done(((f32[1024,64]{0,1:T(8,128)}), f32[1024,64]{0,1:T(8,128)}) %all-reduce.2.cloned.1.call-update) | async-done | bytes 262160 | tf_op jit(solution)/shard_map/psum | solution.py:231
  (1028 shorter events, 586.9 us)
Async XLA Ops:
  7.2 58.8 %copy-start = (bf16[1,128,8192]{2,1,0:T(8,128)(2,1)S(1)}, bf16[1,128,8192]{2,1,0:T(8,128)(2,1)}, u32[]{:S(2)}) copy-start(bf16[1,128,8192]{2,1,0:T(8,128)(2,1)} %param.21) | copy-start | bytes 6291460
  7.2 58.8 %all-gather.8.cloned.1.call-start = ((), (), s32[]{:S(2)}) async-start(), calls=%async_computation.4 | async-start | bytes 1179648 | tf_op jit(solution)/shard_map/all_gather | solution.py:35
  7.9 174.1 %all-gather.6.cloned.1.call-start = ((), (), s32[]{:S(2)}) async-start(), calls=%async_computation.3 | async-start | bytes 9437184 | tf_op jit(solution)/shard_map/all_gather | solution.py:34
  8.7 240.9 %all-gather.12.cloned.1.call-start = ((), (), s32[]{:S(2)}) async-start(), calls=%async_computation.7 | async-start | bytes 4325376 | tf_op jit(solution)/shard_map/all_gather | solution.py:189
  9.4 308.9 %all-gather.10.cloned.1.call-start = ((), (), s32[]{:S(2)}) async-start(), calls=%async_computation.5 | async-start | bytes 4325376 | tf_op jit(solution)/shard_map/all_gather | solution.py:188
  39.6 147.1 %copy-start.16 = (bf16[64,512]{0,1:T(8,128)(2,1)}, bf16[64,512]{0,1:T(8,128)(2,1)S(1)}, u32[]{:S(2)}) copy-start(bf16[64,512]{0,1:T(8,128)(2,1)S(1)} %all_gather.17) | copy-start | bytes 196612
  68.1 118.6 %copy-start.21 = (bf16[128,64]{0,1:T(8,128)(2,1)}, bf16[128,64]{0,1:T(8,128)(2,1)S(1)}, u32[]{:S(2)}) copy-start(bf16[128,64]{0,1:T(8,128)(2,1)S(1)} %fusion.80) | copy-start | bytes 49156
  68.1 119.6 %copy-start.1 = (s32[1,64]{1,0:T(1,128)S(1)}, s32[1,64]{1,0:T(1,128)}, u32[]{:S(2)}) copy-start(s32[1,64]{1,0:T(1,128)} %param.28) | copy-start | bytes 772
  68.1 121.0 %copy-start.2 = (s32[1,4096]{1,0:T(1,128)S(1)}, s32[1,4096]{1,0:T(1,128)}, u32[]{:S(2)}) copy-start(s32[1,4096]{1,0:T(1,128)} %param.29) | copy-start | bytes 49156
  186.7 3.6 copy-start.19
  187.6 1125.5 %reduce-scatter.6.cloned.1.call-start = ((), (), s32[]{:S(2)}) async-start(), calls=%async_computation.6 | async-start | bytes 8650752 | tf_op jit(solution)/shard_map/reduce_scatter | solution.py:212
  590.9 16.5 copy-start.6
  616.9 3.2 copy-start.11
  621.2 4.9 copy-start.7
  626.1 16.5 copy-start.6
  643.7 3.2 copy-start.11
  648.1 4.9 copy-start.7
  653.0 16.5 copy-start.6
  670.6 3.2 copy-start.11
  674.9 4.9 copy-start.7
  679.9 16.5 copy-start.6
  697.5 3.2 copy-start.11
  701.8 4.9 copy-start.7
  706.7 16.5 copy-start.6
  726.9 3.2 copy-start.11
  731.2 5.0 copy-start.7
  736.2 16.5 copy-start.6
  762.2 3.2 copy-start.11
  766.5 5.0 copy-start.7
  771.4 16.5 copy-start.6
  791.6 3.2 copy-start.11
  795.9 4.9 copy-start.7
  800.8 16.5 copy-start.6
  818.4 3.2 copy-start.11
  822.7 5.0 copy-start.7
  827.8 16.5 copy-start.6
  845.4 3.2 copy-start.11
  849.7 5.0 copy-start.7
  854.7 16.5 copy-start.6
  874.9 3.2 copy-start.11
  879.2 5.0 copy-start.7
  884.2 16.5 copy-start.6
  901.8 3.2 copy-start.11
  906.1 4.9 copy-start.7
  911.0 16.5 copy-start.6
  934.5 3.2 copy-start.11
  938.8 5.0 copy-start.7
  943.8 16.5 copy-start.6
  961.4 3.2 copy-start.11
  965.7 4.9 copy-start.7
  970.6 16.5 copy-start.6
  988.3 3.2 copy-start.11
  992.6 4.9 copy-start.7
  997.5 16.5 copy-start.6
  1015.1 3.2 copy-start.11
  1019.5 5.0 copy-start.7
  1024.4 16.5 copy-start.6
  1042.0 3.2 copy-start.11
  1046.4 4.9 copy-start.7
  1060.4 252.8 %copy-start.17 = (bf16[64,512]{0,1:T(8,128)(2,1)S(1)}, bf16[64,512]{0,1:T(8,128)(2,1)}, u32[]{:S(2)}) copy-start(bf16[64,512]{0,1:T(8,128)(2,1)} %copy-done.16) | copy-start | bytes 196612
  1060.4 337.8 %reduce-scatter.8.cloned.1.call-start = ((), (), s32[]{:S(2)}) async-start(), calls=%async_computation.8 | async-start | bytes 2359296 | tf_op jit(solution)/shard_map/reduce_scatter | solution.py:233
  1316.1 160.6 %reduce-scatter.10.cloned.1.call-start = ((), (), s32[]{:S(2)}) async-start(), calls=%async_computation.10 | async-start | bytes 294912
  1320.9 77.2 %copy-start.14 = (bf16[8192,64]{0,1:T(8,128)(2,1)S(1)}, bf16[8192,64]{0,1:T(8,128)(2,1)}, u32[]{:S(2)}) copy-start(bf16[8192,64]{0,1:T(8,128)(2,1)} %all-gather.8.cloned.1.call-done) | copy-start | bytes 3145732
  1320.9 381.9 %all-reduce.2.cloned.1.call-start = ((), (), s32[]{:S(2)}) async-start(), calls=%async_computation.9 | async-start | bytes 524288 | tf_op jit(solution)/shard_map/psum | solution.py:231
  (82 other events, 141.6 us)
Sparse Core Ops, SparseCore 0:
  10.6 55.2 all-gather.7
  68.6 113.3 all-gather.5
  183.9 65.5 all-gather.11
  251.8 66.4 all-gather.9
  1060.5 252.5 reduce-scatter.5
  1317.0 81.0 reduce-scatter.7
  1403.1 73.5 reduce-scatter.9
  1479.3 223.4 all-reduce.1
where the time goes:
time: 1720 us; the launch traced here: 1710 us
  waiting for transfers between devices  779 us (45%)
  local copies, waits for them, and re-layouts  493 us (29%)
  other arithmetic  153 us (9%)
  blocking collectives  133 us (8%)
  matrix products  73.1 us (4%)
  loops' own time  66.2 us (4%)
    reduce_scatter x1, waiting for transfers between devices, body(): lax.psum_scatter(key_sums.astype(jnp.bfloat16), 'context', scatter_dimens...  253 us
    psum x1, waiting for transfers between devices, body(): summed = lax.psum((down_resident, up_resident), 'context')  122 us
    all_gather x1, waiting for transfers between devices, body(): lax.all_gather(key_base_weight, 'fsdp', axis=0, tiled=True)  114 us
    psum x1, blocking collectives, body(): summed = lax.psum((down_resident, up_resident), 'context')  104 us
    dynamic_update_slice x32, local copies, waits for them, and re-layouts, second_pass(): lax.dynamic_update_slice_in_dim(key_sums, previous + key_terms, start, 0)  79.1 us
    dynamic_slice x32, local copies, waits for them, and re-layouts, second_pass(): previous = lax.dynamic_slice_in_dim(key_sums, start, key_total_count, 0)  77.4 us
    dynamic_slice x64, local copies, waits for them, and re-layouts, run_blocks(): lax.scan(block_step, init, (block_ids, block_keys, block_values))  76.6 us
    unnamed x9, waiting for transfers between devices  75.7 us
  transfers between devices with their start and end apart: 8, of which 8 were waited for; matrix products, arithmetic and copies ran while one was open for 2% of the time, Pallas kernels for 0%

commit v1 on v0

v1 whole, which is shorter than its diff:
```python
import functools
import math

import jax
import jax.numpy as jnp
from jax import lax
from jax.experimental import pallas as pl
from jax.experimental.pallas import tpu as pltpu
from jax.sharding import PartitionSpec as P

QUERY_HEADS = 32
KEY_VALUE_HEADS = 4
HEAD_SIZE = 128
GROUPS = QUERY_HEADS // KEY_VALUE_HEADS
SPAN = 64
ADAPTER_SCALE = 0.5
NEGATIVE_FILL = -1e30
KEY_TILE = 256
MESH = pl.DeviceIdType.MESH
ANY = pl.BlockSpec(memory_space=pl.ANY)
VMEM = pl.BlockSpec(memory_space=pltpu.VMEM)
SMEM = pl.BlockSpec(memory_space=pltpu.SMEM)


def at(start, size):
    return pl.ds(pl.multiple_of(start, size), size)


class Place:
    def __init__(self, zs):
        self.zs = zs
        self.fsdp = lax.axis_index("fsdp")
        self.context = lax.axis_index("context")
        self.y_hi, self.x = lax.div(self.fsdp, 4), lax.rem(self.fsdp, 4)
        self.z, self.member = lax.div(self.context, 4), lax.rem(self.context, 4)
        self.y_lo, self.core = lax.div(self.member, 2), lax.rem(self.member, 2)

    def row(self, y_hi, x):
        return y_hi * 4 + lax.rem(x, 4)

    def at_x(self, step):
        return {"fsdp": self.row(self.y_hi, self.x + step), "context": self.context}

    def across_y(self):
        return {
            "fsdp": self.row(1 - self.y_hi, self.x),
            "context": self.z * 4 + (1 - self.y_lo) * 2 + self.core,
        }

    def other_y_lo(self):
        return self.of_context(self.z * 4 + (1 - self.y_lo) * 2 + self.core)

    def sibling(self):
        return self.of_context(self.z * 4 + self.y_lo * 2 + 1 - self.core)

    def of_context(self, context):
        return {"fsdp": self.fsdp, "context": context}

    def fellow(self, k):
        return lax.rem(self.member + k, 4)

    def at_fellow(self, k):
        return self.of_context(self.z * 4 + self.fellow(k))

    def z_at(self, step):
        return lax.rem(self.z + step + self.zs, self.zs)

    def at_z(self, step):
        return self.of_context(self.z_at(step) * 4 + self.member)


def greet(partners):
    barrier = pltpu.get_barrier_semaphore()
    for partner in partners:
        pl.semaphore_signal(barrier, inc=1, device_id=partner, device_id_type=MESH)
    pl.semaphore_wait(barrier, len(partners))


class Sender:
    def __init__(self, send_sems, recv_sems):
        self.send_sems, self.recv_sems, self.copies = send_sems, recv_sems, []

    def send(self, src, dst, device):
        k = len(self.copies)
        assert k < self.send_sems.shape[0]
        copy = pltpu.make_async_remote_copy(
            src_ref=src,
            dst_ref=dst,
            send_sem=self.send_sems.at[k],
            recv_sem=self.recv_sems.at[k],
            device_id=device,
            device_id_type=MESH,
        )
        copy.start()
        self.copies.append(copy)
        return copy

    def finish(self):
        for copy in self.copies:
            copy.wait_send()


def ring_gather(place, sender, buffer, rows):
    half = place.zs // 2
    last_right = last_left = None
    for step in range(half):
        if last_right is not None:
            last_right.wait_recv()
            last_left.wait_recv()
        right_at, left_at = place.z_at(-step) * rows, place.z_at(step) * rows
        if step < half - 1:
            right_rows, left_rows = at(right_at, rows), at(left_at, rows)
        else:
            cut = rows // 2
            right_rows, left_rows = at(right_at, cut), at(left_at + cut, cut)
        last_right = sender.send(buffer.at[right_rows], buffer.at[right_rows], place.at_z(1))
        last_left = sender.send(buffer.at[left_rows], buffer.at[left_rows], place.at_z(-1))
        yield
    last_right.wait_recv()
    last_left.wait_recv()


def weights_kernel(
    zs, w_ref, q_ref, g_ref, v_ref, wf_ref, qg_ref, gg_ref, vg_ref, send_sems, recv_sems, own_sems
):
    place = Place(zs)
    tokens = q_ref.shape[0]
    shard = w_ref.shape[0]
    piece, part = shard // 2, shard // 4
    width = GROUPS * HEAD_SIZE
    member = place.member
    owns = [
        pltpu.make_async_copy(w_ref, wf_ref.at[at(place.fsdp * shard, shard)], own_sems.at[0]),
        pltpu.make_async_copy(
            q_ref.at[:, at(member * width, width)], qg_ref.at[at(member * tokens, tokens)], own_sems.at[1]
        ),
        pltpu.make_async_copy(
            g_ref.at[:, at(member * width, width)], gg_ref.at[at(member * tokens, tokens)], own_sems.at[2]
        ),
        pltpu.make_async_copy(
            v_ref.at[:, at(member * HEAD_SIZE, HEAD_SIZE)],
            vg_ref.at[at((place.z * 4 + member) * tokens, tokens)],
            own_sems.at[3],
        ),
    ]
    for own in owns:
        own.start()
    right, left, across, sibling = place.at_x(1), place.at_x(3), place.across_y(), place.sibling()
    greet([right, left, across] + [place.at_fellow(k) for k in (1, 2, 3)] + [place.at_z(1), place.at_z(-1)])
    sender = Sender(send_sems, recv_sems)
    send = sender.send

    value_copies = []
    for k in (1, 2, 3):
        fellow = place.fellow(k)
        value_copies.append(
            send(
                v_ref.at[:, at(fellow * HEAD_SIZE, HEAD_SIZE)],
                vg_ref.at[at((place.z * 4 + member) * tokens, tokens)],
                place.at_fellow(k),
            )
        )

    def rows_of(y_hi, x, offset, size):
        return wf_ref.at[at(place.row(y_hi, x) * shard + place.core * piece + offset, size)]

    y_hi, other, x = place.y_hi, 1 - place.y_hi, place.x
    own_piece = w_ref.at[at(place.core * piece, piece)]
    landing = rows_of(y_hi, x, 0, piece)
    to_right = send(own_piece, landing, right)
    to_left = send(own_piece, landing, left)
    to_across = send(own_piece, landing, across)
    head_copies = []
    for k in (2, 3, 1):
        fellow = place.fellow(k)
        for src, dst in ((q_ref, qg_ref), (g_ref, gg_ref)):
            head_copies.append(
                send(
                    src.at[:, at(fellow * width, width)],
                    dst.at[at(member * tokens, tokens)],
                    place.at_fellow(k),
                )
            )
    for copy in value_copies:
        copy.wait_recv()
    owns[3].wait()
    ring = ring_gather(place, sender, vg_ref, 4 * tokens)
    next(ring)

    shared = []

    def share(block):
        shared.append(send(block, block, sibling))

    to_right.wait_recv()
    half_right = send(rows_of(y_hi, x + 3, 0, part), rows_of(y_hi, x + 3, 0, part), right)
    to_left.wait_recv()
    half_left = send(rows_of(y_hi, x + 1, part, part), rows_of(y_hi, x + 1, part, part), left)
    share(rows_of(y_hi, x + 3, 0, piece))
    share(rows_of(y_hi, x + 1, 0, piece))
    to_across.wait_recv()
    block = rows_of(other, x, 0, piece)
    on_right = send(block, block, right)
    on_left = send(block, block, left)
    share(block)
    next(ring, None)
    half_right.wait_recv()
    block = rows_of(y_hi, x + 2, 0, part)
    first_across = send(block, block, across)
    share(block)
    half_left.wait_recv()
    block = rows_of(y_hi, x + 2, part, part)
    second_across = send(block, block, across)
    share(block)
    for _ in ring:
        pass
    on_right.wait_recv()
    share(rows_of(other, x + 3, 0, piece))
    on_left.wait_recv()
    share(rows_of(other, x + 1, 0, piece))
    first_across.wait_recv()
    share(rows_of(other, x + 2, 0, part))
    second_across.wait_recv()
    share(rows_of(other, x + 2, part, part))
    for copy in head_copies + shared:
        copy.wait_recv()
    sender.finish()
    for own in owns[:3]:
        own.wait()


def keys_kernel(zs, k_ref, kg_ref, send_sems, recv_sems, own_sem):
    place = Place(zs)
    tokens = k_ref.shape[0]
    member = place.member
    mine = at((place.z * 4 + member) * tokens, tokens)
    own = pltpu.make_async_copy(k_ref.at[:, at(member * HEAD_SIZE, HEAD_SIZE)], kg_ref.at[mine], own_sem)
    own.start()
    greet([place.at_fellow(k) for k in (1, 2, 3)] + [place.at_z(1), place.at_z(-1)])
    sender = Sender(send_sems, recv_sems)
    copies = []
    for k in (1, 2, 3):
        fellow = place.fellow(k)
        copies.append(
            sender.send(
                k_ref.at[:, at(fellow * HEAD_SIZE, HEAD_SIZE)], kg_ref.at[mine], place.at_fellow(k)
            )
        )
    for copy in copies:
        copy.wait_recv()
    own.wait()
    for _ in ring_gather(place, sender, kg_ref, 4 * tokens):
        pass
    sender.finish()


def attention_kernel(
    slot_ref,
    first_ref,
    inverse_ref,
    pos_ref,
    start_ref,
    q_ref,
    g_ref,
    k_ref,
    v_ref,
    dq_ref,
    dkv_ref,
    keys,
    values,
    totals,
    scores,
    grads,
):
    inv_root = 1.0 / math.sqrt(HEAD_SIZE)
    lanes = GROUPS * SPAN
    spans = inverse_ref.shape[0]

    @pl.loop(0, spans)
    def _(n):
        src, dst = at(inverse_ref[n] * SPAN, SPAN), at(n * SPAN, SPAN)
        keys[dst, :] = k_ref[src, :]
        values[dst, :] = v_ref[src, :]
        totals[dst, :] = jnp.zeros((SPAN, 2 * HEAD_SIZE), jnp.float32)

    @pl.loop(0, slot_ref.shape[0])
    def _(i):
        slot, first = slot_ref[i], first_ref[i]
        own = at(i * SPAN, SPAN)
        q_rows = jnp.concatenate(
            [q_ref[own, g * HEAD_SIZE : (g + 1) * HEAD_SIZE] for g in range(GROUPS)], axis=0
        )
        g_rows = jnp.concatenate(
            [g_ref[own, g * HEAD_SIZE : (g + 1) * HEAD_SIZE] for g in range(GROUPS)], axis=0
        )
        q_pos, q_start = pos_ref[pl.ds(i, 1), :], start_ref[pl.ds(i, 1), :]
        low_tile = lax.div(first * SPAN, KEY_TILE)
        tiles = lax.div(slot * SPAN, KEY_TILE) - low_tile + 1

        def rows_at(t):
            return at((low_tile + t) * KEY_TILE, KEY_TILE)

        def peak_step(t, peak):
            rows = rows_at(t)
            raw = lax.dot_general(
                keys[rows, :], q_rows, (((1,), (1,)), ((), ())), preferred_element_type=jnp.float32
            )
            key_pos = (low_tile + t) * KEY_TILE + lax.broadcasted_iota(jnp.int32, (KEY_TILE, lanes), 0)
            raw = jnp.where((key_pos >= q_start) & (key_pos <= q_pos), raw * inv_root, NEGATIVE_FILL)
            scores[t] = raw
            return jnp.maximum(peak, jnp.max(raw, axis=0, keepdims=True))

        peak = lax.fori_loop(0, tiles, peak_step, jnp.full((1, lanes), NEGATIVE_FILL, jnp.float32))

        def sum_step(t, carry):
            normalizer, weighted = carry
            grad_prob = lax.dot_general(
                values[rows_at(t), :], g_rows, (((1,), (1,)), ((), ())), preferred_element_type=jnp.float32
            )
            weights = jnp.exp(scores[t] - peak)
            scores[t] = weights
            grads[t] = grad_prob
            return (
                normalizer + jnp.sum(weights, axis=0, keepdims=True),
                weighted + jnp.sum(weights * grad_prob, axis=0, keepdims=True),
            )

        zero = jnp.zeros((1, lanes), jnp.float32)
        normalizer, weighted = lax.fori_loop(0, tiles, sum_step, (zero, zero))
        inverse = 1.0 / normalizer
        row_terms = weighted * inverse

        def grad_step(t, dq):
            rows = rows_at(t)
            probability = scores[t] * inverse
            dscore = (probability * (grads[t] - row_terms) * inv_root).astype(jnp.bfloat16)
            prob_low = probability.astype(jnp.bfloat16)
            totals[rows, :HEAD_SIZE] += jnp.dot(dscore, q_rows, preferred_element_type=jnp.float32)
            totals[rows, HEAD_SIZE:] += jnp.dot(prob_low, g_rows, preferred_element_type=jnp.float32)
            return dq + lax.dot_general(
                keys[rows, :], dscore, (((0,), (0,)), ((), ())), preferred_element_type=jnp.float32
            )

        dq = lax.fori_loop(0, tiles, grad_step, jnp.zeros((HEAD_SIZE, lanes), jnp.float32))
        dq = dq.T.astype(jnp.bfloat16)
        for g in range(GROUPS):
            dq_ref[own, g * HEAD_SIZE : (g + 1) * HEAD_SIZE] = dq[g * SPAN : (g + 1) * SPAN]

    @pl.loop(0, spans)
    def _(n):
        dkv_ref[at(inverse_ref[n] * SPAN, SPAN), :] = totals[at(n * SPAN, SPAN), :].astype(jnp.bfloat16)


REDUCE_CUTS = 2


def reduce_plan(zs):
    half = zs // 2
    return [(1, 0, half), (-1, 1, half), (-1, 0, half - 1), (1, 1, half - 1)]


def reduce_kernel(zs, dkv_ref, dqg_ref, dq_ref, kg_ref, vg_ref, out, held, done, send_sems, recv_sems, own_sems):
    place = Place(zs)
    tokens = dq_ref.shape[0]
    width = GROUPS * HEAD_SIZE
    member = place.member
    rows = 4 * tokens
    cut = rows // REDUCE_CUTS
    own_query = pltpu.make_async_copy(
        dqg_ref.at[at(member * tokens, tokens)], dq_ref.at[:, at(member * width, width)], own_sems.at[0]
    )
    own_query.start()
    greet([place.at_fellow(k) for k in (1, 2, 3)] + [place.at_z(1), place.at_z(-1)])
    sender = Sender(send_sems, recv_sems)
    plan = reduce_plan(zs)
    last = {}
    slot = 0
    query_copies = []
    for step in range(zs // 2):
        for piece in range(REDUCE_CUTS):
            for chain, (direction, column, hops) in enumerate(plan):
                if step >= hops:
                    continue
                columns = slice(column * HEAD_SIZE, (column + 1) * HEAD_SIZE)
                destination = place.z_at(direction * (hops - step))
                mine = dkv_ref[at(destination * rows + piece * cut, cut), columns]
                if step > 0:
                    copy, before = last[chain, piece]
                    copy.wait_recv()
                    mine = (mine.astype(jnp.float32) + held[before].astype(jnp.float32)).astype(jnp.bfloat16)
                out[slot] = mine
                last[chain, piece] = (
                    sender.send(out.at[slot], held.at[slot], place.at_z(direction)),
                    slot,
                )
                slot += 1
        if step == 0:
            for k in (2, 3, 1):
                fellow = place.fellow(k)
                query_copies.append(
                    sender.send(
                        dqg_ref.at[at(fellow * tokens, tokens)],
                        dq_ref.at[:, at(member * width, width)],
                        place.at_fellow(k),
                    )
                )
    for piece in range(REDUCE_CUTS):
        for column in range(2):
            columns = slice(column * HEAD_SIZE, (column + 1) * HEAD_SIZE)
            total = dkv_ref[at(place.z * rows + piece * cut, cut), columns].astype(jnp.float32)
            for chain, (direction, its_column, hops) in enumerate(plan):
                if its_column == column and hops:
                    copy, before = last[chain, piece]
                    copy.wait_recv()
                    total = total + held[before].astype(jnp.float32)
            done[column, piece * cut : (piece + 1) * cut, :] = total.astype(jnp.bfloat16)
    sums = []
    for column, target in ((0, kg_ref), (1, vg_ref)):
        own = pltpu.make_async_copy(
            done.at[column, at(member * tokens, tokens)],
            target.at[:, at(member * HEAD_SIZE, HEAD_SIZE)],
            own_sems.at[1 + column],
        )
        own.start()
        sums.append(own)
    copies = []
    for k in (2, 3, 1):
        for column, target in ((0, kg_ref), (1, vg_ref)):
            copies.append(
                sender.send(
                    done.at[column, at(place.fellow(k) * tokens, tokens)],
                    target.at[:, at(member * HEAD_SIZE, HEAD_SIZE)],
                    place.at_fellow(k),
                )
            )
    for copy in copies + query_copies:
        copy.wait_recv()
    sender.finish()
    for own in sums + [own_query]:
        own.wait()


def adapter_kernel(
    zs, part_ref, total_ref, pair_in, row_out, row_in, y_out, y_in, z_out, z_in, lo_out, lo_in, send_sems, recv_sems
):
    place = Place(zs)
    lanes = part_ref.shape[3] - 128
    cut = lanes // zs
    sibling, across, other_lo = place.sibling(), place.across_y(), place.other_y_lo()
    partners = [place.at_x(k) for k in (1, 2, 3)] + [across, other_lo]
    partners += [place.at_z(k) for k in range(1, zs)]
    partners += [
        place.of_context(place.z_at(k) * 4 + place.y_lo * 2 + 1 - place.core) for k in range(zs)
    ]
    greet(partners)
    sender = Sender(send_sems, recv_sems)
    send = sender.send
    copy = send(part_ref.at[:, 1 - place.core], pair_in, sibling)
    copy.wait_recv()
    row_out[...] = (
        part_ref[:, pl.ds(place.core, 1)][:, 0].astype(jnp.float32) + pair_in[...].astype(jnp.float32)
    ).astype(jnp.bfloat16)
    copies = []
    for k in (2, 1, 3):
        for y_hi in range(2):
            copies.append(
                send(
                    row_out.at[place.row(y_hi, place.x + k)], row_in.at[k - 1, y_hi], place.at_x(k)
                )
            )
    for copy in copies:
        copy.wait_recv()

    def over_x(y_hi):
        total = row_out[place.row(y_hi, place.x)].astype(jnp.float32)
        for k in range(3):
            total = total + row_in[k, y_hi].astype(jnp.float32)
        return total

    y_out[...] = over_x(1 - place.y_hi)
    copy = send(y_out, y_in, across)
    mine = over_x(place.y_hi)
    copy.wait_recv()
    mine = mine + y_in[...]
    for j in range(zs):
        z_out[j, 0] = mine[:, j * cut : (j + 1) * cut]
        z_out[j, 1] = mine[:, lanes:]
    copies = []
    for k in sorted(range(1, zs), key=lambda k: -min(k, zs - k)):
        copies.append(send(z_out.at[place.z_at(k)], z_in.at[k - 1], place.at_z(k)))
    for copy in copies:
        copy.wait_recv()
    chunk = z_out[place.z]
    for k in range(zs - 1):
        chunk = chunk + z_in[k]
    lo_out[...] = chunk
    copy = send(lo_out, lo_in, other_lo)
    copy.wait_recv()
    chunk = chunk + lo_in[...]
    total_ref[pl.ds(place.core, 1), pl.ds(place.z, 1)] = chunk[0][None, None]
    total_ref[pl.ds(place.core, 1), zs : zs + 1] = chunk[1][None, None]
    copies = [
        send(total_ref.at[place.core, zs], total_ref.at[place.core, zs], sibling),
    ]
    block = total_ref.at[place.core, place.z]
    for k in sorted(range(zs), key=lambda k: -min(k, zs - k)):
        if k:
            copies.append(send(block, block, place.at_z(k)))
        copies.append(
            send(block, block, place.of_context(place.z_at(k) * 4 + place.y_lo * 2 + 1 - place.core))
        )
    for copy in copies:
        copy.wait_recv()
    sender.finish()


def dma(count):
    return pltpu.SemaphoreType.DMA((count,))


def params(collective_id=None):
    if collective_id is None:
        return pltpu.CompilerParams(vmem_limit_bytes=56 << 20)
    return pltpu.CompilerParams(
        vmem_limit_bytes=48 << 20, collective_id=collective_id, has_side_effects=True
    )


def body(
    zs,
    inputs,
    queries,
    values,
    output_gradient,
    key_base_weight,
    adapter_down,
    adapter_up,
    span_slot_index,
    segment_document,
):
    bf16, f32, i32 = jnp.bfloat16, jnp.float32, jnp.int32
    rows_in = inputs[0]
    tokens, model = rows_in.shape
    shard, kv_width = key_base_weight.shape
    rank = adapter_down.shape[1]
    length = segment_document.shape[1]
    width = GROUPS * HEAD_SIZE
    half = zs // 2

    up_block = jnp.pad(adapter_up, ((0, shard - rank), (0, 0)))
    packed = jnp.concatenate([key_base_weight, adapter_down, up_block], axis=1)
    packed_width = packed.shape[1]
    full, query_group, gradient_group, value_all = pl.pallas_call(
        functools.partial(weights_kernel, zs),
        out_shape=(
            jax.ShapeDtypeStruct((model, packed_width), bf16),
            jax.ShapeDtypeStruct((4 * tokens, width), bf16),
            jax.ShapeDtypeStruct((4 * tokens, width), bf16),
            jax.ShapeDtypeStruct((length, HEAD_SIZE), bf16),
        ),
        in_specs=[ANY] * 4,
        out_specs=(ANY,) * 4,
        scratch_shapes=[dma(27 + 2 * half), dma(27 + 2 * half), dma(4)],
        compiler_params=params(0),
        name="gather_weights",
    )(packed, queries[0], output_gradient[0], values[0])

    projected = jnp.dot(rows_in, full, preferred_element_type=f32)
    low_rank = projected[:, kv_width : kv_width + rank].astype(bf16)
    up_blocks = full.reshape(8, shard, packed_width)[:, :rank, kv_width + rank :]
    complete_up = up_blocks.transpose(1, 0, 2).reshape(rank, kv_width)
    key_matrix = (
        projected[:, :kv_width]
        + ADAPTER_SCALE * jnp.dot(low_rank, complete_up, preferred_element_type=f32)
    ).astype(bf16)

    key_all = pl.pallas_call(
        functools.partial(keys_kernel, zs),
        out_shape=jax.ShapeDtypeStruct((length, HEAD_SIZE), bf16),
        in_specs=[ANY],
        out_specs=ANY,
        scratch_shapes=[dma(3 + 2 * half), dma(3 + 2 * half), pltpu.SemaphoreType.DMA],
        compiler_params=params(1),
        name="gather_keys",
    )(key_matrix)

    listing, documents = span_slot_index[0], segment_document[0]
    spans = listing.shape[0]
    z = lax.axis_index("context") // 4
    own_spans = 4 * tokens // SPAN
    slots = lax.dynamic_slice_in_dim(listing, z * own_spans, own_spans, 0)
    span_ids = jnp.arange(spans, dtype=i32)
    inverse = jnp.sum(jnp.where(listing[None, :] == span_ids[:, None], span_ids[None, :], 0), axis=1)
    own_docs = documents.reshape(spans, SPAN)[slots]
    starts = jnp.sum((documents[None, None, :] < own_docs[:, :, None]).astype(i32), axis=2)
    positions = slots[:, None] * SPAN + jnp.arange(SPAN, dtype=i32)[None, :]
    query_grad_group, partial_sums = pl.pallas_call(
        attention_kernel,
        out_shape=(
            jax.ShapeDtypeStruct((4 * tokens, width), bf16),
            jax.ShapeDtypeStruct((length, 2 * HEAD_SIZE), bf16),
        ),
        in_specs=[SMEM] * 3 + [VMEM] * 6,
        out_specs=(VMEM, VMEM),
        scratch_shapes=[
            pltpu.VMEM((length, HEAD_SIZE), bf16),
            pltpu.VMEM((length, HEAD_SIZE), bf16),
            pltpu.VMEM((length, 2 * HEAD_SIZE), f32),
            pltpu.VMEM((1024 // KEY_TILE + 2, KEY_TILE, GROUPS * SPAN), f32),
            pltpu.VMEM((1024 // KEY_TILE + 2, KEY_TILE, GROUPS * SPAN), f32),
        ],
        compiler_params=params(),
        name="attention_gradients",
    )(
        slots,
        starts[:, 0] // SPAN,
        inverse,
        jnp.tile(positions, (1, GROUPS)),
        jnp.tile(starts, (1, GROUPS)),
        query_group,
        gradient_group,
        key_all,
        value_all,
    )

    hops = REDUCE_CUTS * sum(hops for _, _, hops in reduce_plan(zs))
    cut = 4 * tokens // REDUCE_CUTS
    query_grad, key_gradient, value_grad = pl.pallas_call(
        functools.partial(reduce_kernel, zs),
        out_shape=(
            jax.ShapeDtypeStruct((tokens, QUERY_HEADS * HEAD_SIZE), bf16),
            jax.ShapeDtypeStruct((tokens, kv_width), bf16),
            jax.ShapeDtypeStruct((tokens, kv_width), bf16),
        ),
        in_specs=[VMEM, ANY],
        out_specs=(ANY,) * 3,
        scratch_shapes=[
            pltpu.VMEM((hops, cut, HEAD_SIZE), bf16),
            pltpu.VMEM((hops, cut, HEAD_SIZE), bf16),
            pltpu.VMEM((2, 4 * tokens, HEAD_SIZE), bf16),
            dma(hops + 9),
            dma(hops + 9),
            dma(3),
        ],
        compiler_params=params(2),
        name="reduce_keys_values",
    )(partial_sums, query_grad_group)

    key_lifted = lax.dot_general(
        key_gradient, complete_up, (((1,), (1,)), ((), ())), preferred_element_type=f32
    ).astype(bf16)
    scaled_lifted = (key_lifted.astype(f32) * ADAPTER_SCALE).astype(bf16)
    stacked = jnp.concatenate([key_gradient, scaled_lifted, jnp.zeros_like(key_lifted)], axis=1)
    down_part = lax.dot_general(
        scaled_lifted, rows_in, (((0,), (0,)), ((), ())), preferred_element_type=f32
    ).astype(bf16)
    up_part = ADAPTER_SCALE * lax.dot_general(
        low_rank, key_gradient, (((0,), (0,)), ((), ())), preferred_element_type=f32
    )
    share = kv_width // 8
    down_part = down_part.reshape(2, rank // 2, 8, shard).transpose(2, 0, 1, 3)
    up_part = up_part.astype(bf16).reshape(2, rank // 2, 8, share).transpose(2, 0, 1, 3)
    up_part = jnp.pad(up_part, ((0, 0), (0, 0), (0, 0), (0, 128 - share)))
    parts = jnp.concatenate([down_part, up_part], axis=3)
    lanes = shard + 128
    chunk = shard // zs
    ranks = rank // 2
    copies = 1 + 6 + 1 + (zs - 1) + 1 + 1 + 2 * zs - 1
    totals = pl.pallas_call(
        functools.partial(adapter_kernel, zs),
        out_shape=jax.ShapeDtypeStruct((2, zs + 1, ranks, chunk), f32),
        in_specs=[VMEM],
        out_specs=VMEM,
        scratch_shapes=[
            pltpu.VMEM((8, ranks, lanes), bf16),
            pltpu.VMEM((8, ranks, lanes), bf16),
            pltpu.VMEM((3, 2, ranks, lanes), bf16),
            pltpu.VMEM((ranks, lanes), f32),
            pltpu.VMEM((ranks, lanes), f32),
            pltpu.VMEM((zs, 2, ranks, chunk), f32),
            pltpu.VMEM((zs - 1, 2, ranks, chunk), f32),
            pltpu.VMEM((2, ranks, chunk), f32),
            pltpu.VMEM((2, ranks, chunk), f32),
            dma(copies),
            dma(copies),
        ],
        compiler_params=params(3),
        name="sum_adapter_gradients",
    )(parts)
    input_gradient = lax.dot_general(
        stacked, full, (((1,), (1,)), ((), ())), preferred_element_type=f32
    ).astype(bf16)
    down_share = totals[:, :zs].transpose(1, 3, 0, 2).reshape(shard, rank)
    up_share = totals[:, zs, :, :share].reshape(rank, share)
    return (query_grad[None], value_grad[None], input_gradient[None], down_share, up_share)


def solution(mesh):
    spread, rows = P("fsdp", "context", None), P("fsdp", None)
    placed = (spread, spread, spread, spread, rows, rows, P(None, "fsdp"), rows, rows)
    return jax.shard_map(
        functools.partial(body, mesh.shape["context"] // 4),
        mesh=mesh,
        in_specs=placed,
        out_specs=(spread, spread, spread, rows, P(None, "fsdp")),
        check_vma=False,
    )
```

time: 1720 us -> 212 us (0.12)
  waiting for transfers between devices: 779 us -> 0 us
  local copies, waits for them, and re-layouts: 493 us -> 15.5 us
  Pallas kernels: 0 us -> 167 us
  other arithmetic: 153 us -> 9.86 us
  blocking collectives: 133 us -> 0 us
  loops' own time: 66.2 us -> 0 us
  matrix products: 73.1 us -> 18 us
    reduce_scatter x2 -> x0, waiting for transfers between devices: 322 us -> none  [the longest x1 253 us: body(): lax.psum_scatter(key_sums.astype(jnp.bfloat16), 'context', scatter_dimens...]
    all_gather x4 -> x0, waiting for transfers between devices: 260 us -> none  [the longest x1 114 us: body(): lax.all_gather(key_base_weight, 'fsdp', axis=0, tiled=True)]
    pallas_call x0 -> x5, Pallas kernels: none -> 167 us  [the longest x1 51.9 us: body(): pl.pallas_call(functools.partial(weights_kernel, zs), out_shape=(jax.Shap...]
    dynamic_slice x96 -> x0, local copies, waits for them, and re-layouts: 154 us -> none  [the longest x32 77.4 us: second_pass(): previous = lax.dynamic_slice_in_dim(key_sums, start, key_total_count, 0)]
    psum x1 -> x0, waiting for transfers between devices: 122 us -> none  [body(): summed = lax.psum((down_resident, up_resident), 'context')]
    gather x66 -> x1, local copies, waits for them, and re-layouts: 117 us -> 0.55 us  [body(): own_docs = documents.reshape(spans, SPAN)[slots]]
    psum x1 -> x0, blocking collectives: 104 us -> none  [body(): summed = lax.psum((down_resident, up_resident), 'context')]
    another operation x72 -> x0, other arithmetic: 80.5 us -> none  [the longest x16 51.1 us: second_pass(): return (jnp.stack(query_parts), key_sums)]
  transfers between devices with their start and end apart: 8 -> 0, of which waited for: 8 -> 0; matrix products, arithmetic and copies ran while one was open for 2% -> 0% of each run, Pallas kernels for 0% -> 0%
where the time goes in v1:
time: 212 us; the launch traced here: 211 us
  Pallas kernels  167 us (79%)
  matrix products  18 us (8%)
  local copies, waits for them, and re-layouts  15.5 us (7%)
  other arithmetic  9.86 us (5%)
    pallas_call x1, Pallas kernels, body(): pl.pallas_call(functools.partial(weights_kernel, zs), out_shape=(jax.Shap...  51.9 us
    pallas_call x1, Pallas kernels, body(): pl.pallas_call(functools.partial(adapter_kernel, zs), out_shape=jax.Shape...  39.9 us
    pallas_call x1, Pallas kernels, body(): pl.pallas_call(functools.partial(reduce_kernel, zs), out_shape=(jax.Shape...  31.3 us
    pallas_call x1, Pallas kernels, body(): pl.pallas_call(attention_kernel, out_shape=(jax.ShapeDtypeStruct((4 * tok...  22.1 us
    pallas_call x1, Pallas kernels, body(): pl.pallas_call(functools.partial(keys_kernel, zs), out_shape=jax.ShapeDty...  21.6 us
    unnamed x35, local copies, waits for them, and re-layouts  8.68 us
    dot_general x1, matrix products, body(): lax.dot_general(stacked, full, (((1,), (1,)), ((), ())), preferred_elemen...  8.68 us
    dot_general x1, matrix products, body(): projected = jnp.dot(rows_in, full, preferred_element_type=f32)  6.9 us

profile of v1, /device:TPU:1, one launch (start us, length us, event | category | flops | bytes accessed | tf_op | source)
XLA Modules:
  0.0 211.1 jit_solution(1168129192653155496)
XLA Ops:
  0.6 0.0 copy-start
  0.6 0.0 copy-start.3
  0.7 0.0 copy-start.9
  0.7 0.9 fusion.22
  1.6 0.5 broadcast.90
  2.1 1.4 reduce.5
  3.5 0.1 reshape_squeeze.6
  3.6 0.6 gather_fusion
  4.1 1.7 convert_reduce_fusion
  5.8 0.1 slice_reduce_fusion
  5.9 1.2 broadcast_multiply_fusion
  7.2 0.1 iota_add_fusion
  7.3 0.7 tile.9.pos_ref
  8.0 0.7 tile.21.start_ref
  8.6 1.1 copy.33
  9.7 0.0 copy-start.4
  9.7 2.5 %fusion.6.w_ref = bf16[1024,640]{1,0:T(8,128)(2,1)} fusion(bf16[64,64]{1,0:T(8,128)(2,1)} %param.15, bf16[1024,64]{1,0:T(8,128)(2,1)S(1)} %copy.33, bf16[1024,512]{1,0:T(8,128)(2,1)} %param.13), kind=kLoop, calls=%fused_computation.12 | loop fusion | flops 5242880 | bytes 2498560 | tf_op jit(solution)/shard_map/concatenate | solution.py:551
  12.2 0.0 copy-done.3
  12.2 0.0 copy-done.9
  12.2 0.0 copy-done.4
  12.2 51.9 %gather_weights.1 = (bf16[8192,640]{1,0:T(8,128)(2,1)}, bf16[512,1024]{1,0:T(8,128)(2,1)S(1)}, bf16[512,1024]{1,0:T(8,128)(2,1)S(1)}, bf16[4096,128]{1,0:T(8,128)(2,1)S(1)}) custom-call(bf16[1024,640]{1,0:T(8,128)(2,1)} %fusion.6.w_ref, bf16[128,4096]{1,0:T(8,128)(2,1)S(1)} %bitcast.55, bf16[128,4096]{1,0:T(8,128)(2,1)S(1)} %bitcast.56, ...), custom_call_target="tpu_custom_call" | custom-call | tf_op jit(solution)/shard_map/gather_weights/pallas_call | solution.py:553
  64.1 0.0 copy-start.5
  64.1 0.0 copy-start.6
  64.1 0.0 copy-start.7
  64.1 0.0 copy-done
  64.2 6.9 %fusion.7 = f32[128,640]{1,0:T(8,128)S(1)} fusion(bf16[8192,640]{1,0:T(8,128)(2,1)} %get-tuple-element.16, bf16[1,128,8192]{2,1,0:T(8,128)(2,1)S(1)} %copy-done), kind=kOutput, calls=%fused_computation.13 | convolution fusion | flops 1342177280 | bytes 12910592 | tf_op jit(solution)/shard_map/dot_general | solution.py:568
  71.1 0.0 copy-done.5
  71.1 0.0 copy-done.6
  71.1 0.0 copy-done.7
  71.1 0.0 copy-start.10
  71.1 0.0 copy-start.13
  71.1 1.1 slice.29
  72.3 0.1 copy.51
  72.4 0.1 reshape.90
  72.5 0.2 fusion.12.k_ref
  72.7 21.6 %gather_keys.1.k_ref = bf16[4096,128]{1,0:T(8,128)(2,1)S(1)} custom-call(bf16[128,512]{1,0:T(8,128)(2,1)S(1)} %fusion.12.k_ref), custom_call_target="tpu_custom_call" | custom-call | tf_op jit(solution)/shard_map/gather_keys/pallas_call | solution.py:577
  94.3 0.0 copy-start.1
  94.3 1.0 copy-done.1
  95.3 0.0 copy-done.13
  95.3 0.7 select_reduce_fusion.inverse_ref
  96.0 22.1 %attention_gradients.1 = (bf16[512,1024]{1,0:T(8,128)(2,1)}, bf16[4096,256]{1,0:T(8,128)(2,1)}) custom-call(s32[8]{0:T(128)} %get-tuple-element.24.slot_ref, s32[8]{0:T(128)} %get-tuple-element.25.first_ref, s32[64]{0:T(128)} %select_reduce_fusion.inverse_ref, s32[8,512]{1,0:T(8,128)} %tile.9.pos_ref, s32[8,512]{1,0:T(8,128)} %tile.21.start_ref, ...), custom_call_target="tpu_custom_call" | custom-call | tf_op jit(solution)/shard_map/attention_gradients/pallas_call | solution.py:597
  118.1 0.0 copy-done.10
  118.1 1.6 copy-done.2
  119.7 1.2 copy-done.8
  120.9 31.3 %reduce_keys_values.1 = (bf16[128,4096]{1,0:T(8,128)(2,1)S(1)}, bf16[128,512]{1,0:T(8,128)(2,1)S(1)}, bf16[128,512]{1,0:T(8,128)(2,1)S(1)}) custom-call(bf16[4096,256]{1,0:T(8,128)(2,1)S(1)} %copy-done.2, bf16[512,1024]{1,0:T(8,128)(2,1)S(1)} %copy-done.8), custom_call_target="tpu_custom_call" | custom-call | tf_op jit(solution)/shard_map/reduce_keys_values/pallas_call | solution.py:628
  152.2 0.2 fusion.16
  152.4 0.0 copy-start.11
  152.4 0.5 convolution_convert_fusion.1
  152.9 0.1 copy-done.11
  153.0 0.6 copy.43
  153.6 1.5 copy.49
  155.2 1.7 fusion.13
  156.8 1.0 reshape.92
  157.9 1.3 fusion.10.part_ref
  159.2 0.0 copy-start.12
  159.2 39.9 %sum_adapter_gradients.1 = f32[2,9,32,128]{3,2,1,0:T(8,128)S(1)} custom-call(bf16[8,2,32,1152]{3,2,1,0:T(8,128)(2,1)S(1)} %fusion.10.part_ref), custom_call_target="tpu_custom_call" | custom-call | tf_op jit(solution)/shard_map/sum_adapter_gradients/pallas_call | solution.py:669
  199.2 0.2 copy.39
  199.3 0.8 copy.50
  200.1 0.6 slice.24
  200.7 0.1 pad.14.clone
  200.8 0.0 copy-done.12
  200.8 8.7 %fusion = bf16[1,128,8192]{2,1,0:T(8,128)(2,1)} fusion(bf16[8192,640]{1,0:T(8,128)(2,1)} %get-tuple-element.16, bf16[128,64]{1,0:T(8,128)(2,1)S(1)} %copy-done.12, bf16[128,512]{1,0:T(8,128)(2,1)S(1)} %get-tuple-element.22, bf16[640]{0:T(1024)(128)(2,1)S(1)} %pad.14.clone), kind=kOutput, calls=%fused_computation.2 | convolution fusion | flops 1343717376 | bytes 12731648 | tf_op jit(solution)/shard_map/dot_general | solution.py:690
  209.5 1.0 copy.55
  210.5 0.7 copy.56
  (8 shorter events, 0.1 us)
Async XLA Ops:
  0.6 63.5 %copy-start = (bf16[1,128,8192]{2,1,0:T(8,128)(2,1)S(1)}, bf16[1,128,8192]{2,1,0:T(8,128)(2,1)}, u32[]{:S(2)}) copy-start(bf16[1,128,8192]{2,1,0:T(8,128)(2,1)} %param.9) | copy-start | bytes 6291460
  0.6 11.6 %copy-start.3 = (bf16[1,128,4096]{2,1,0:T(8,128)(2,1)S(1)}, bf16[1,128,4096]{2,1,0:T(8,128)(2,1)}, u32[]{:S(2)}) copy-start(bf16[1,128,4096]{2,1,0:T(8,128)(2,1)} %param.10) | copy-start | bytes 3145732
  0.7 11.6 %copy-start.9 = (bf16[1,128,512]{2,1,0:T(8,128)(2,1)S(1)}, bf16[1,128,512]{2,1,0:T(8,128)(2,1)}, u32[]{:S(2)}) copy-start(bf16[1,128,512]{2,1,0:T(8,128)(2,1)} %param.11) | copy-start | bytes 393220
  9.7 2.5 %copy-start.4 = (bf16[1,128,4096]{2,1,0:T(8,128)(2,1)S(1)}, bf16[1,128,4096]{2,1,0:T(8,128)(2,1)}, u32[]{:S(2)}) copy-start(bf16[1,128,4096]{2,1,0:T(8,128)(2,1)} %param.12) | copy-start | bytes 3145732
  64.1 6.9 %copy-start.5 = (bf16[512,1024]{1,0:T(8,128)(2,1)}, bf16[512,1024]{1,0:T(8,128)(2,1)S(1)}, u32[]{:S(2)}) copy-start(bf16[512,1024]{1,0:T(8,128)(2,1)S(1)} %get-tuple-element.14.q_ref) | copy-start | bytes 3145732
  64.1 6.9 %copy-start.6 = (bf16[512,1024]{1,0:T(8,128)(2,1)}, bf16[512,1024]{1,0:T(8,128)(2,1)S(1)}, u32[]{:S(2)}) copy-start(bf16[512,1024]{1,0:T(8,128)(2,1)S(1)} %get-tuple-element.15.g_ref) | copy-start | bytes 3145732
  64.1 6.9 %copy-start.7 = (bf16[4096,128]{1,0:T(8,128)(2,1)}, bf16[4096,128]{1,0:T(8,128)(2,1)S(1)}, u32[]{:S(2)}) copy-start(bf16[4096,128]{1,0:T(8,128)(2,1)S(1)} %get-tuple-element.17.v_ref) | copy-start | bytes 3145732
  71.1 47.0 %copy-start.10 = (f32[128,640]{1,0:T(8,128)}, f32[128,640]{1,0:T(8,128)S(1)}, u32[]{:S(2)}) copy-start(f32[128,640]{1,0:T(8,128)S(1)} %fusion.7) | copy-start | bytes 983044
  71.1 24.2 %copy-start.13 = (s32[1,64]{1,0:T(1,128)S(1)}, s32[1,64]{1,0:T(1,128)}, u32[]{:S(2)}) copy-start(s32[1,64]{1,0:T(1,128)} %param.16) | copy-start | bytes 772
  94.3 1.0 copy-start.1
  118.1 1.6 copy-start.2
  119.7 1.2 copy-start.8
  152.4 0.6 copy-start.11
  159.2 41.6 %copy-start.12 = (bf16[128,64]{1,0:T(8,128)(2,1)S(1)}, bf16[128,64]{1,0:T(8,128)(2,1)}, u32[]{:S(2)}) copy-start(bf16[128,64]{1,0:T(8,128)(2,1)} %copy-done.11) | copy-start | bytes 49156

commit v2 on v1

v2 whole, which is shorter than its diff:
```python
import functools
import math

import jax
import jax.numpy as jnp
from jax import lax
from jax.experimental import pallas as pl
from jax.experimental.pallas import tpu as pltpu
from jax.sharding import PartitionSpec as P

QUERY_HEADS = 32
KEY_VALUE_HEADS = 4
HEAD_SIZE = 128
GROUPS = QUERY_HEADS // KEY_VALUE_HEADS
SPAN = 64
ADAPTER_SCALE = 0.5
NEGATIVE_FILL = -1e30
KEY_TILE = 256
MESH = pl.DeviceIdType.MESH
ANY = pl.BlockSpec(memory_space=pl.ANY)
VMEM = pl.BlockSpec(memory_space=pltpu.VMEM)
SMEM = pl.BlockSpec(memory_space=pltpu.SMEM)


def at(start, size):
    return pl.ds(pl.multiple_of(start, size), size)


class Place:
    def __init__(self, zs):
        self.zs = zs
        self.fsdp = lax.axis_index("fsdp")
        self.context = lax.axis_index("context")
        self.y_hi, self.x = lax.div(self.fsdp, 4), lax.rem(self.fsdp, 4)
        self.z, self.member = lax.div(self.context, 4), lax.rem(self.context, 4)
        self.y_lo, self.core = lax.div(self.member, 2), lax.rem(self.member, 2)

    def row(self, y_hi, x):
        return y_hi * 4 + lax.rem(x, 4)

    def at_x(self, step):
        return {"fsdp": self.row(self.y_hi, self.x + step), "context": self.context}

    def across_y(self):
        return {
            "fsdp": self.row(1 - self.y_hi, self.x),
            "context": self.z * 4 + (1 - self.y_lo) * 2 + self.core,
        }

    def other_y_lo(self):
        return self.of_context(self.z * 4 + (1 - self.y_lo) * 2 + self.core)

    def sibling(self):
        return self.of_context(self.z * 4 + self.y_lo * 2 + 1 - self.core)

    def of_context(self, context):
        return {"fsdp": self.fsdp, "context": context}

    def fellow(self, k):
        return lax.rem(self.member + k, 4)

    def at_fellow(self, k):
        return self.of_context(self.z * 4 + self.fellow(k))

    def z_at(self, step):
        return lax.rem(self.z + step + self.zs, self.zs)

    def at_z(self, step):
        return self.of_context(self.z_at(step) * 4 + self.member)


def greet(partners):
    barrier = pltpu.get_barrier_semaphore()
    for partner in partners:
        pl.semaphore_signal(barrier, inc=1, device_id=partner, device_id_type=MESH)
    pl.semaphore_wait(barrier, len(partners))


class Sender:
    def __init__(self, send_sems, recv_sems):
        self.send_sems, self.recv_sems, self.copies = send_sems, recv_sems, []

    def send(self, src, dst, device):
        k = len(self.copies)
        assert k < self.send_sems.shape[0]
        copy = pltpu.make_async_remote_copy(
            src_ref=src,
            dst_ref=dst,
            send_sem=self.send_sems.at[k],
            recv_sem=self.recv_sems.at[k],
            device_id=device,
            device_id_type=MESH,
        )
        copy.start()
        self.copies.append(copy)
        return copy

    def finish(self):
        for copy in self.copies:
            copy.wait_send()


class Ring:
    def __init__(self, place, sender, buffer, block, rows):
        self.place, self.sender, self.buffer = place, sender, buffer
        self.block, self.rows, self.stage, self.flying = block, rows, 0, ()
        self.stages = place.zs // 2

    def step(self):
        for copy in self.flying:
            copy.wait_recv()
        self.flying = ()
        if self.stage == self.stages:
            return
        right_at, left_at = self.block(self.place.z_at(-self.stage)), self.block(self.place.z_at(self.stage))
        if self.stage < self.stages - 1:
            right_rows, left_rows = at(right_at, self.rows), at(left_at, self.rows)
        else:
            cut = self.rows // 2
            right_rows, left_rows = at(right_at, cut), at(left_at + cut, cut)
        buffer, send = self.buffer, self.sender.send
        self.flying = (
            send(buffer.at[right_rows], buffer.at[right_rows], self.place.at_z(1)),
            send(buffer.at[left_rows], buffer.at[left_rows], self.place.at_z(-1)),
        )
        self.stage += 1

    def run(self):
        while self.stage < self.stages or self.flying:
            self.step()


def keys_kernel(
    zs,
    w_ref,
    d_ref,
    u_ref,
    x_hbm,
    q_ref,
    g_ref,
    v_ref,
    full_ref,
    qg_ref,
    gg_ref,
    vg_ref,
    kg_ref,
    low_ref,
    up_ref,
    full,
    inputs,
    projected,
    keys,
    send_sems,
    recv_sems,
    own_sems,
):
    place = Place(zs)
    tokens = q_ref.shape[0]
    shard, kv_width = w_ref.shape
    rank = d_ref.shape[1]
    unit = shard // 8
    width = GROUPS * HEAD_SIZE
    member = place.member
    mine = at((place.z * 4 + member) * tokens, tokens)
    columns = at(member * HEAD_SIZE, HEAD_SIZE)
    load = pltpu.make_async_copy(x_hbm, inputs, own_sems.at[0])
    load.start()
    owns = [
        pltpu.make_async_copy(
            q_ref.at[:, at(member * width, width)], qg_ref.at[at(member * tokens, tokens)], own_sems.at[1]
        ),
        pltpu.make_async_copy(
            g_ref.at[:, at(member * width, width)], gg_ref.at[at(member * tokens, tokens)], own_sems.at[2]
        ),
        pltpu.make_async_copy(v_ref.at[:, columns], vg_ref.at[mine], own_sems.at[3]),
    ]
    for own in owns:
        own.start()
    own_rows = at(place.fsdp * shard, shard)
    full[own_rows, :kv_width] = w_ref[...]
    up_rows = jnp.concatenate([u_ref[...], jnp.zeros((shard - rank, u_ref.shape[1]), jnp.bfloat16)], axis=0)
    full[own_rows, kv_width:] = jnp.concatenate([d_ref[...], up_rows], axis=1)
    projected[...] = jnp.zeros_like(projected)

    right, left, across, sibling = place.at_x(1), place.at_x(3), place.across_y(), place.sibling()
    z_up, z_down = place.at_z(1), place.at_z(-1)
    greet([right, left, across] + [place.at_fellow(k) for k in (1, 2, 3)] + [z_up, z_down])
    sender = Sender(send_sems, recv_sems)
    send = sender.send

    parity = lax.rem(place.z, 2)

    def rows_of(f, offset, size):
        begin = f * shard + place.core * 4 * unit + offset
        return full.at[pl.ds(pl.multiple_of(begin, unit // 2), size)]

    def main(f):
        return rows_of(f, parity * unit, 3 * unit)

    def pass_on(block, *devices):
        return [send(block, block, device) for device in devices]

    half = 3 * unit // 2

    def first_half(f):
        return rows_of(f, parity * unit, half)

    def second_half(f):
        return rows_of(f, parity * unit + half, half)

    y_hi, x = place.y_hi, place.x
    row = lambda y, step: place.row(y, x + step)
    own, near_left, near_right, far = (row(y_hi, k) for k in (0, 3, 1, 2))
    over, over_left, over_right, over_far = (row(1 - y_hi, k) for k in (0, 3, 1, 2))

    value_copies = [
        send(
            v_ref.at[:, at(place.fellow(k) * HEAD_SIZE, HEAD_SIZE)], vg_ref.at[mine], place.at_fellow(k)
        )
        for k in (1, 2, 3)
    ]
    from_left, from_right, from_over = pass_on(main(own), right, left, across)
    head_copies = []
    for k in (2, 3, 1):
        for src, dst in ((q_ref, qg_ref), (g_ref, gg_ref)):
            head_copies.append(
                send(
                    src.at[:, at(place.fellow(k) * width, width)],
                    dst.at[at(member * tokens, tokens)],
                    place.at_fellow(k),
                )
            )

    shares = {}
    crossing = {}

    def share(name, block):
        shares.setdefault(name, []).extend(pass_on(block, sibling))

    def cross(name, f):
        bridge = parity * 3 * unit
        crossing[name] = (
            pass_on(rows_of(f, bridge, unit // 2), z_up)
            + pass_on(rows_of(f, bridge + unit // 2, unit // 2), z_down)
        )

    def land(name, f):
        for copy in crossing[name]:
            copy.wait_recv()
        share(name, rows_of(f, (1 - parity) * 3 * unit, unit))

    def project(name, f):
        for copy in shares.get(name, ()):
            copy.wait_recv()

        @pl.loop(0, 2)
        def _(part):
            rows = at(f * shard + part * (shard // 2), shard // 2)
            projected[...] += jnp.dot(inputs[:, rows], full[rows, :], preferred_element_type=jnp.float32)

    load.wait()
    project("own", own)
    for copy in value_copies:
        copy.wait_recv()
    owns[2].wait()
    ring = Ring(place, sender, vg_ref, lambda z: z * 4 * tokens, 4 * tokens)
    ring.step()

    from_left.wait_recv()
    far_first = pass_on(first_half(near_left), right)[0]
    from_right.wait_recv()
    far_second = pass_on(second_half(near_right), left)[0]
    from_over.wait_recv()
    over_from_left, over_from_right = pass_on(main(over), right, left)
    for name, f in (("near_left", near_left), ("near_right", near_right), ("over", over)):
        share(name, main(f))
        cross(name, f)
    ring.step()
    far_first.wait_recv()
    over_far_first = pass_on(first_half(far), across)[0]
    far_second.wait_recv()
    over_far_second = pass_on(second_half(far), across)[0]
    share("far", main(far))
    cross("far", far)
    ring.step()
    for name, f in (("near_left", near_left), ("near_right", near_right), ("over", over)):
        land(name, f)
    project("near_left", near_left)
    project("near_right", near_right)
    land("far", far)
    ring.run()
    project("over", over)
    over_from_left.wait_recv()
    share("over_left", main(over_left))
    cross("over_left", over_left)
    over_from_right.wait_recv()
    share("over_right", main(over_right))
    cross("over_right", over_right)
    project("far", far)
    over_far_first.wait_recv()
    over_far_second.wait_recv()
    share("over_far", main(over_far))
    cross("over_far", over_far)
    land("over_left", over_left)
    land("over_right", over_right)
    project("over_left", over_left)
    project("over_right", over_right)
    land("over_far", over_far)
    project("over_far", over_far)
    store = pltpu.make_async_copy(full, full_ref, own_sems.at[0])
    store.start()

    low_rank = projected[:, kv_width : kv_width + rank].astype(jnp.bfloat16)
    low_ref[...] = low_rank
    for f in range(8):
        up_ref[:, f * (kv_width // 8) : (f + 1) * (kv_width // 8)] = full[
            f * shard : f * shard + rank, kv_width + rank :
        ]
    keys[...] = (
        projected[:, :kv_width]
        + ADAPTER_SCALE * jnp.dot(low_rank, up_ref[...], preferred_element_type=jnp.float32)
    ).astype(jnp.bfloat16)
    own_keys = pltpu.make_async_copy(keys.at[:, columns], kg_ref.at[mine], own_sems.at[4])
    own_keys.start()

    def exchange(device, fellow):
        return send(keys.at[:, at(fellow * HEAD_SIZE, HEAD_SIZE)], kg_ref.at[mine], device)

    to_sibling = exchange(sibling, member + 1 - 2 * place.core)
    other = [
        exchange(place.at_fellow(k), place.fellow(k)) for k in (2,)
    ]
    third = lax.rem(member + 3 - 2 * place.core, 4)
    other.append(exchange(place.of_context(place.z * 4 + third), third))
    rings = [
        Ring(place, sender, kg_ref, lambda z: (z * 4 + place.y_lo * 2) * tokens, 2 * tokens),
        Ring(place, sender, kg_ref, lambda z: (z * 4 + (1 - place.y_lo) * 2) * tokens, 2 * tokens),
    ]
    to_sibling.wait_recv()
    own_keys.wait()
    rings[0].step()
    for copy in other:
        copy.wait_recv()
    rings[1].step()
    while any(ring.flying for ring in rings):
        for ring in rings:
            ring.step()
    for copy in head_copies:
        copy.wait_recv()
    sender.finish()
    owns[0].wait()
    owns[1].wait()
    store.wait()


def attention_kernel(
    zs,
    list_ref,
    doc_smem,
    doc_ref,
    q_hbm,
    g_hbm,
    k_hbm,
    v_hbm,
    dq_hbm,
    dkv_hbm,
    queries,
    gradients,
    keys,
    values,
    totals,
    scores,
    grads,
    dq_rows,
    rounded,
    firsts,
    starts,
    load_sems,
    store_sems,
):
    to_exponent = math.log2(math.e) / math.sqrt(HEAD_SIZE)
    inv_root = 1.0 / math.sqrt(HEAD_SIZE)
    lanes = GROUPS * SPAN
    spans = list_ref.shape[0]
    own_spans = queries.shape[0] // SPAN
    z = lax.div(lax.axis_index("context"), 4)
    length = spans * SPAN

    loads = [
        pltpu.make_async_copy(q_hbm, queries, load_sems.at[0]),
        pltpu.make_async_copy(g_hbm, gradients, load_sems.at[1]),
    ]
    for load in loads:
        load.start()

    def span_copies(s):
        src, dst = at(s * SPAN, SPAN), at(list_ref[s] * SPAN, SPAN)
        return (
            pltpu.make_async_copy(k_hbm.at[src], keys.at[dst], load_sems.at[2]),
            pltpu.make_async_copy(v_hbm.at[src], values.at[dst], load_sems.at[3]),
        )

    @pl.loop(0, spans)
    def _(s):
        for load in span_copies(s):
            load.start()

    keys[length:, :] = jnp.zeros((KEY_TILE, HEAD_SIZE), jnp.bfloat16)
    values[length:, :] = jnp.zeros((KEY_TILE, HEAD_SIZE), jnp.bfloat16)

    @pl.loop(0, spans + KEY_TILE // SPAN)
    def _(n):
        totals[at(n * SPAN, SPAN), :] = jnp.zeros((SPAN, 2 * HEAD_SIZE), jnp.float32)

    def document_start(position):
        document = doc_smem[0, position]

        def narrow(_, carry):
            low, high = carry
            middle = lax.shift_right_logical(low + high, 1)
            earlier = doc_smem[0, middle] < document
            return jnp.where(earlier, middle + 1, low), jnp.where(earlier, high, middle)

        return lax.fori_loop(0, 12, narrow, (jnp.maximum(position - 1024, 0), position))[0]

    shape = (own_spans, 2 * SPAN)
    row = lax.broadcasted_iota(jnp.int32, shape, 0)
    lane = lax.broadcasted_iota(jnp.int32, shape, 1)
    row_begin, row_first = jnp.zeros(shape, jnp.int32), jnp.zeros(shape, jnp.int32)
    for i in range(own_spans):
        slot = list_ref[z * own_spans + i]
        begin = lax.shift_right_logical(slot, 1) * 2 * SPAN
        starts[i : i + 1, :] = doc_ref[0:1, pl.ds(pl.multiple_of(begin, 2 * SPAN), 2 * SPAN)]
        row_begin = jnp.where(row == i, begin, row_begin)
        row_first = jnp.where(row == i, document_start(begin), row_first)
        firsts[i] = lax.shift_right_logical(document_start(slot * SPAN), 6)
    documents = starts[...]
    changes = jnp.where((lane > 0) & (documents != pltpu.roll(documents, 1, 1)), lane, 0)
    for step in (1, 2, 4, 8, 16, 32, 64):
        changes = jnp.maximum(changes, jnp.where(lane >= step, pltpu.roll(changes, step, 1), 0))
    starts[...] = jnp.where(changes == 0, row_first, row_begin + changes)

    for load in loads:
        load.wait()

    pltpu.make_async_copy(k_hbm, keys.at[:length], load_sems.at[2]).wait()
    pltpu.make_async_copy(v_hbm, values.at[:length], load_sems.at[3]).wait()

    @pl.loop(0, own_spans)
    def _(i):
        slot, first = list_ref[z * own_spans + i], firsts[i]
        own = at(i * SPAN, SPAN)
        q_rows = jnp.concatenate(
            [queries[own, g * HEAD_SIZE : (g + 1) * HEAD_SIZE] for g in range(GROUPS)], axis=0
        )
        g_rows = jnp.concatenate(
            [gradients[own, g * HEAD_SIZE : (g + 1) * HEAD_SIZE] for g in range(GROUPS)], axis=0
        )
        pair = starts[pl.ds(i, 1), :]
        own_start = jnp.where(lax.rem(slot, 2) == 1, pair[:, SPAN:], pair[:, :SPAN])
        q_start = jnp.concatenate([own_start] * GROUPS, axis=1) - first * SPAN
        lane = lax.broadcasted_iota(jnp.int32, (1, lanes), 1)
        q_pos = (slot - first) * SPAN + lax.rem(lane, SPAN)
        tiles = lax.div(slot - first + KEY_TILE // SPAN, KEY_TILE // SPAN)

        def rows_at(t, first=first):
            return pl.ds(pl.multiple_of(first * SPAN + t * KEY_TILE, SPAN), KEY_TILE)

        def peak_step(t, peak, q_rows=q_rows, q_start=q_start, q_pos=q_pos, rows_at=rows_at):
            raw = lax.dot_general(
                keys[rows_at(t), :], q_rows, (((1,), (1,)), ((), ())), preferred_element_type=jnp.float32
            )
            key_pos = lax.broadcasted_iota(jnp.int32, (KEY_TILE, lanes), 0)
            raw = jnp.where(
                (key_pos >= q_start - t * KEY_TILE) & (key_pos <= q_pos - t * KEY_TILE), raw, NEGATIVE_FILL
            )
            scores[t] = raw
            grads[t] = lax.dot_general(
                values[rows_at(t), :], g_rows, (((1,), (1,)), ((), ())), preferred_element_type=jnp.float32
            )
            return jnp.maximum(peak, jnp.max(raw, axis=0, keepdims=True))

        peak = lax.fori_loop(0, tiles, peak_step, jnp.full((1, lanes), NEGATIVE_FILL, jnp.float32))

        def sum_step(t, carry, peak=peak):
            normalizer, weighted = carry
            weights = jnp.exp2((scores[t] - peak) * to_exponent)
            scores[t] = weights
            return (
                normalizer + jnp.sum(weights, axis=0, keepdims=True),
                weighted + jnp.sum(weights * grads[t], axis=0, keepdims=True),
            )

        zero = jnp.zeros((1, lanes), jnp.float32)
        normalizer, weighted = lax.fori_loop(0, tiles, sum_step, (zero, zero))
        inverse = 1.0 / normalizer
        row_terms = weighted * inverse

        def grad_step(t, dq, q_rows=q_rows, g_rows=g_rows, inverse=inverse, row_terms=row_terms, rows_at=rows_at):
            rows = rows_at(t)
            probability = scores[t] * inverse
            dscore = (probability * (grads[t] - row_terms) * inv_root).astype(jnp.bfloat16)
            prob_low = probability.astype(jnp.bfloat16)
            totals[rows, :HEAD_SIZE] += jnp.dot(dscore, q_rows, preferred_element_type=jnp.float32)
            totals[rows, HEAD_SIZE:] += jnp.dot(prob_low, g_rows, preferred_element_type=jnp.float32)
            return dq + lax.dot_general(
                keys[rows, :], dscore, (((0,), (0,)), ((), ())), preferred_element_type=jnp.float32
            )

        dq = lax.fori_loop(0, tiles, grad_step, jnp.zeros((HEAD_SIZE, lanes), jnp.float32))
        dq = dq.T.astype(jnp.bfloat16)
        for g in range(GROUPS):
            dq_rows[own, g * HEAD_SIZE : (g + 1) * HEAD_SIZE] = dq[g * SPAN : (g + 1) * SPAN]
        pltpu.make_async_copy(dq_rows.at[own], dq_hbm.at[own], store_sems.at[0]).start()

    @pl.loop(0, spans)
    def _(s):
        rows = at(s * SPAN, SPAN)
        rounded[rows, :] = totals[at(list_ref[s] * SPAN, SPAN), :].astype(jnp.bfloat16)
        pltpu.make_async_copy(rounded.at[rows], dkv_hbm.at[rows], store_sems.at[1]).start()

    pltpu.make_async_copy(dq_rows, dq_hbm, store_sems.at[0]).wait()
    pltpu.make_async_copy(rounded, dkv_hbm, store_sems.at[1]).wait()


REDUCE_CUTS = 2


def reduce_plan(zs):
    half = zs // 2
    return [(1, 0, half), (-1, 1, half), (-1, 0, half - 1), (1, 1, half - 1)]


def finish_kernel(
    zs,
    dkv_ref,
    dqg_ref,
    low_ref,
    up_ref,
    x_hbm,
    full_hbm,
    dq_ref,
    vg_ref,
    grad_ref,
    total_ref,
    out,
    held,
    done,
    key_grad,
    inputs,
    full,
    stacked,
    parts,
    pair_in,
    row,
    far_in,
    near_out,
    near_in,
    y_out,
    y_in,
    z_out,
    z_in,
    lo_out,
    lo_in,
    send_sems,
    recv_sems,
    own_sems,
):
    place = Place(zs)
    tokens = dq_ref.shape[0]
    width = GROUPS * HEAD_SIZE
    member = place.member
    rows = 4 * tokens
    cut = rows // REDUCE_CUTS
    loads = [
        pltpu.make_async_copy(x_hbm, inputs, own_sems.at[0]),
        pltpu.make_async_copy(full_hbm, full, own_sems.at[1]),
    ]
    for load in loads:
        load.start()
    own_query = pltpu.make_async_copy(
        dqg_ref.at[at(member * tokens, tokens)], dq_ref.at[:, at(member * width, width)], own_sems.at[2]
    )
    own_query.start()
    right, left, across = place.at_x(1), place.at_x(3), place.across_y()
    sibling, other_lo = place.sibling(), place.other_y_lo()
    greet(
        [place.at_fellow(k) for k in (1, 2, 3)]
        + [place.at_z(k) for k in range(1, zs)]
        + [right, left, across]
    )
    sender = Sender(send_sems, recv_sems)
    send = sender.send

    plan = reduce_plan(zs)
    last = {}
    slot = 0
    query_copies = []
    for step in range(zs // 2):
        for piece in range(REDUCE_CUTS):
            for chain, (direction, column, hops) in enumerate(plan):
                if step >= hops:
                    continue
                columns = slice(column * HEAD_SIZE, (column + 1) * HEAD_SIZE)
                destination = place.z_at(direction * (hops - step))
                mine = dkv_ref[at(destination * rows + piece * cut, cut), columns]
                if step > 0:
                    copy, before = last[chain, piece]
                    copy.wait_recv()
                    mine = (mine.astype(jnp.float32) + held[before].astype(jnp.float32)).astype(jnp.bfloat16)
                out[slot] = mine
                last[chain, piece] = (send(out.at[slot], held.at[slot], place.at_z(direction)), slot)
                slot += 1
        if step == 0:
            for k in (2, 3, 1):
                query_copies.append(
                    send(
                        dqg_ref.at[at(place.fellow(k) * tokens, tokens)],
                        dq_ref.at[:, at(member * width, width)],
                        place.at_fellow(k),
                    )
                )
    owns, key_copies, value_copies = [], [], []
    for column, target, copies in ((0, key_grad, key_copies), (1, vg_ref, value_copies)):
        columns = slice(column * HEAD_SIZE, (column + 1) * HEAD_SIZE)
        for piece in range(REDUCE_CUTS):
            total = dkv_ref[at(place.z * rows + piece * cut, cut), columns].astype(jnp.float32)
            for chain, (direction, its_column, hops) in enumerate(plan):
                if its_column == column and hops:
                    copy, before = last[chain, piece]
                    copy.wait_recv()
                    total = total + held[before].astype(jnp.float32)
            done[column, piece * cut : (piece + 1) * cut, :] = total.astype(jnp.bfloat16)
        landing = target.at[:, at(member * HEAD_SIZE, HEAD_SIZE)]
        own = pltpu.make_async_copy(
            done.at[column, at(member * tokens, tokens)], landing, own_sems.at[3 + column]
        )
        own.start()
        owns.append(own)
        for k in (2, 3, 1):
            copies.append(
                send(done.at[column, at(place.fellow(k) * tokens, tokens)], landing, place.at_fellow(k))
            )
    loads[0].wait()
    owns[0].wait()
    for copy in key_copies:
        copy.wait_recv()

    kg = key_grad[...]
    lifted = lax.dot_general(
        kg, up_ref[...], (((1,), (1,)), ((), ())), preferred_element_type=jnp.float32
    ).astype(jnp.bfloat16)
    scaled = (lifted.astype(jnp.float32) * ADAPTER_SCALE).astype(jnp.bfloat16)
    rank = lifted.shape[1]
    ranks = rank // 2
    kv_width = kg.shape[1]
    stacked[:, :kv_width] = kg
    stacked[:, kv_width:] = jnp.concatenate([scaled, jnp.zeros_like(scaled)], axis=1)
    up_part = (
        ADAPTER_SCALE
        * lax.dot_general(low_ref[...], kg, (((0,), (0,)), ((), ())), preferred_element_type=jnp.float32)
    ).astype(jnp.bfloat16)
    lanes = parts.shape[3] - 128
    share = kv_width // 8
    padding = jnp.zeros((rank, 128 - share), jnp.bfloat16)
    for f in range(8):
        block = jnp.concatenate([up_part[:, f * share : (f + 1) * share], padding], axis=1)
        parts[f, 0, :, lanes:] = block[:ranks]
        parts[f, 1, :, lanes:] = block[ranks:]

    @pl.loop(0, 8)
    def _(f):
        block = lax.dot_general(
            scaled, inputs[:, at(f * lanes, lanes)], (((0,), (0,)), ((), ())), preferred_element_type=jnp.float32
        ).astype(jnp.bfloat16)
        parts[f, 0, :, :lanes] = block[:ranks]
        parts[f, 1, :, :lanes] = block[ranks:]

    pair_copy = send(parts.at[:, 1 - place.core], pair_in, sibling)
    loads[1].wait()

    def input_gradient(begin, end):
        @pl.loop(begin, end)
        def _(j):
            some = at(j * lanes, lanes)
            grad_ref[:, some] = lax.dot_general(
                stacked[...], full[some, :], (((1,), (1,)), ((), ())), preferred_element_type=jnp.float32
            ).astype(jnp.bfloat16)

    input_gradient(0, 2)
    pair_copy.wait_recv()

    def add(*terms):
        total = terms[0].astype(jnp.float32)
        for term in terms[1:]:
            total = total + term.astype(jnp.float32)
        return total

    @pl.loop(0, 8)
    def _(f):
        row[f] = add(parts[f, pl.ds(place.core, 1)][0], pair_in[f]).astype(jnp.bfloat16)

    here = lambda y_hi, step: place.row(y_hi, place.x + step)
    far_copies = [
        send(row.at[here(0, 2)], far_in.at[0], right),
        send(row.at[here(1, 2)], far_in.at[1], left),
    ]
    near_copies = [
        send(row.at[here(1, 1)], near_in.at[0, 1], right),
        send(row.at[here(0, 3)], near_in.at[1, 0], left),
    ]
    input_gradient(2, 3)
    for way, (y_hi, step, device) in enumerate(((0, 1, right), (1, 3, left))):
        far_copies[way].wait_recv()
        near_out[way] = add(row[here(y_hi, step)], far_in[way]).astype(jnp.bfloat16)
        near_copies.append(send(near_out.at[way], near_in.at[way, y_hi], device))
    input_gradient(3, 5)
    for copy in near_copies:
        copy.wait_recv()

    def over_x(y_hi):
        return add(row[here(y_hi, 0)], near_in[0, y_hi], near_in[1, y_hi])

    y_out[...] = over_x(1 - place.y_hi).astype(jnp.bfloat16)
    y_copy = send(y_out, y_in, across)
    mine = over_x(place.y_hi)
    input_gradient(5, 6)
    y_copy.wait_recv()
    mine = add(mine, y_in[...])
    chunk_lanes = lanes // zs
    cuts = min(zs, 4)
    small = ranks // cuts
    for j in range(zs):
        z_out[j, :ranks] = mine[:, j * chunk_lanes : (j + 1) * chunk_lanes]
        z_out[j, ranks:] = mine[(j % cuts) * small : (j % cuts + 1) * small, lanes:]
    z_copies = []
    for k in sorted(range(1, zs), key=lambda k: -min(k, zs - k)):
        z_copies.append(send(z_out.at[place.z_at(k)], z_in.at[k - 1], place.at_z(k)))
    input_gradient(6, 7)
    for copy in z_copies:
        copy.wait_recv()
    chunk = z_out[place.z]
    for k in range(zs - 1):
        chunk = chunk + z_in[k]
    lo_out[...] = chunk
    lo_copy = send(lo_out, lo_in, other_lo)
    lo_copy.wait_recv()
    chunk = chunk + lo_in[...]
    total_ref[pl.ds(place.core, 1), pl.ds(place.z, 1)] = chunk[None, None]
    block = total_ref.at[place.core, place.z]
    z_copies = []
    for k in sorted(range(1, zs), key=lambda k: -min(k, zs - k)):
        z_copies.append(send(block, block, place.at_z(k)))
    input_gradient(7, 8)
    for copy in z_copies:
        copy.wait_recv()
    block = total_ref.at[place.core]
    send(block, block, sibling).wait_recv()
    for copy in value_copies + query_copies:
        copy.wait_recv()
    sender.finish()
    owns[1].wait()
    own_query.wait()


def dma(count):
    return pltpu.SemaphoreType.DMA((count,))


def params(collective_id=None):
    if collective_id is None:
        return pltpu.CompilerParams(vmem_limit_bytes=56 << 20)
    return pltpu.CompilerParams(
        vmem_limit_bytes=48 << 20, collective_id=collective_id, has_side_effects=True
    )


def body(
    zs,
    inputs,
    queries,
    values,
    output_gradient,
    key_base_weight,
    adapter_down,
    adapter_up,
    span_slot_index,
    segment_document,
):
    bf16, f32, i32 = jnp.bfloat16, jnp.float32, jnp.int32
    rows_in = inputs[0]
    tokens, model = rows_in.shape
    shard, kv_width = key_base_weight.shape
    rank = adapter_down.shape[1]
    length = segment_document.shape[1]
    width = GROUPS * HEAD_SIZE
    half = zs // 2
    shape = jax.ShapeDtypeStruct
    packed_width = kv_width + rank + adapter_up.shape[1]

    copies = 3 + 3 + 6 + 2 + 2 + 2 + 7 * 4 + 3 + 3 * 2 * half
    full, query_group, gradient_group, value_all, key_all, low_rank, complete_up = pl.pallas_call(
        functools.partial(keys_kernel, zs),
        out_shape=(
            shape((model, packed_width), bf16),
            shape((4 * tokens, width), bf16),
            shape((4 * tokens, width), bf16),
            shape((length, HEAD_SIZE), bf16),
            shape((length, HEAD_SIZE), bf16),
            shape((tokens, rank), bf16),
            shape((rank, kv_width), bf16),
        ),
        in_specs=[VMEM] * 3 + [ANY] * 4,
        out_specs=(ANY,) * 5 + (VMEM,) * 2,
        scratch_shapes=[
            pltpu.VMEM((model, packed_width), bf16),
            pltpu.VMEM((tokens, model), bf16),
            pltpu.VMEM((tokens, packed_width), f32),
            pltpu.VMEM((tokens, kv_width), bf16),
            dma(copies),
            dma(copies),
            dma(5),
        ],
        compiler_params=params(0),
        name="gather_weights_and_keys",
    )(
        key_base_weight,
        adapter_down,
        adapter_up,
        rows_in,
        queries[0],
        output_gradient[0],
        values[0],
    )

    span_rows = 4 * tokens
    tile_rows = (1024 // KEY_TILE + 1, KEY_TILE, GROUPS * SPAN)
    query_grad_group, partial_sums = pl.pallas_call(
        functools.partial(attention_kernel, zs),
        out_shape=(
            jax.ShapeDtypeStruct((span_rows, width), bf16),
            jax.ShapeDtypeStruct((length, 2 * HEAD_SIZE), bf16),
        ),
        in_specs=[SMEM, SMEM, VMEM] + [ANY] * 4,
        out_specs=(ANY, ANY),
        scratch_shapes=[
            pltpu.VMEM((span_rows, width), bf16),
            pltpu.VMEM((span_rows, width), bf16),
            pltpu.VMEM((length + KEY_TILE, HEAD_SIZE), bf16),
            pltpu.VMEM((length + KEY_TILE, HEAD_SIZE), bf16),
            pltpu.VMEM((length + KEY_TILE, 2 * HEAD_SIZE), f32),
            pltpu.VMEM(tile_rows, f32),
            pltpu.VMEM(tile_rows, f32),
            pltpu.VMEM((span_rows, width), bf16),
            pltpu.VMEM((length, 2 * HEAD_SIZE), bf16),
            pltpu.SMEM((span_rows // SPAN,), i32),
            pltpu.VMEM((span_rows // SPAN, 2 * SPAN), i32),
            dma(4),
            dma(2),
        ],
        compiler_params=params(),
        name="attention_gradients",
    )(
        span_slot_index[0],
        segment_document,
        segment_document,
        query_group,
        gradient_group,
        key_all,
        value_all,
    )

    hops = REDUCE_CUTS * sum(hops for _, _, hops in reduce_plan(zs))
    cut = 4 * tokens // REDUCE_CUTS
    ranks = rank // 2
    lanes = shard + 128
    chunk = (ranks + ranks // min(zs, 4), shard // zs)
    copies = hops + 9 + 1 + 6 + 1 + 2 * (zs - 1) + 2
    query_grad, value_grad, input_gradient, totals = pl.pallas_call(
        functools.partial(finish_kernel, zs),
        out_shape=(
            shape((tokens, QUERY_HEADS * HEAD_SIZE), bf16),
            shape((tokens, kv_width), bf16),
            shape((tokens, model), bf16),
            shape((2, zs) + chunk, f32),
        ),
        in_specs=[VMEM, ANY, VMEM, VMEM, ANY, ANY],
        out_specs=(ANY, ANY, VMEM, VMEM),
        scratch_shapes=[
            pltpu.VMEM((hops, cut, HEAD_SIZE), bf16),
            pltpu.VMEM((hops, cut, HEAD_SIZE), bf16),
            pltpu.VMEM((2, 4 * tokens, HEAD_SIZE), bf16),
            pltpu.VMEM((tokens, kv_width), bf16),
            pltpu.VMEM((tokens, model), bf16),
            pltpu.VMEM((model, packed_width), bf16),
            pltpu.VMEM((tokens, packed_width), bf16),
            pltpu.VMEM((8, 2, ranks, lanes), bf16),
            pltpu.VMEM((8, ranks, lanes), bf16),
            pltpu.VMEM((8, ranks, lanes), bf16),
            pltpu.VMEM((2, ranks, lanes), bf16),
            pltpu.VMEM((2, ranks, lanes), bf16),
            pltpu.VMEM((2, 2, ranks, lanes), bf16),
            pltpu.VMEM((ranks, lanes), bf16),
            pltpu.VMEM((ranks, lanes), bf16),
            pltpu.VMEM((zs,) + chunk, f32),
            pltpu.VMEM((zs - 1,) + chunk, f32),
            pltpu.VMEM(chunk, f32),
            pltpu.VMEM(chunk, f32),
            dma(copies),
            dma(copies),
            dma(5),
        ],
        compiler_params=params(1),
        name="sum_gradients",
    )(partial_sums, query_grad_group, low_rank, complete_up, rows_in, full)

    share = kv_width // 8
    down_share = totals[:, :, :ranks].transpose(1, 3, 0, 2).reshape(shard, rank)
    up_share = totals[:, : min(zs, 4), ranks:, :share].reshape(rank, share)
    return (query_grad[None], value_grad[None], input_gradient[None], down_share, up_share)


def solution(mesh):
    spread, rows = P("fsdp", "context", None), P("fsdp", None)
    placed = (spread, spread, spread, spread, rows, rows, P(None, "fsdp"), rows, rows)
    return jax.shard_map(
        functools.partial(body, mesh.shape["context"] // 4),
        mesh=mesh,
        in_specs=placed,
        out_specs=(spread, spread, spread, rows, P(None, "fsdp")),
        check_vma=False,
    )
```

time: 212 us -> 168 us (0.79)
  matrix products: 18 us -> 0 us
  Pallas kernels: 167 us -> 153 us
  other arithmetic: 9.86 us -> 0 us
    dot_general x6 -> x0, matrix products: 18 us -> none  [the longest x1 8.68 us: body(): lax.dot_general(stacked, full, (((1,), (1,)), ((), ())), preferred_elemen...]
    pallas_call x5 -> x3, Pallas kernels: 167 us -> 153 us  [the longest x1 67.3 us: body(): pl.pallas_call(functools.partial(keys_kernel, zs), out_shape=(shape((mode...]
    unnamed x35 -> x21, local copies, waits for them, and re-layouts: 8.68 us -> 12.8 us
    concatenate x2 -> x0, other arithmetic: 3.84 us -> none  [the longest x1 2.51 us: body(): packed = jnp.concatenate([key_base_weight, adapter_down, up_block], axis=1)]
    reshape x4 -> x0, local copies, waits for them, and re-layouts: 2.69 us -> none  [the longest x1 1.55 us: body(): down_part = down_part.reshape(2, rank // 2, 8, shard).transpose(2, 0, 1, 3)]
    reduce_sum x2 -> x0, other arithmetic: 2.4 us -> none  [the longest x1 1.7 us: body(): jnp.sum((documents[None, None, :] < own_docs[:, :, None]).astype(i32), ax...]
where the time goes in v2:
time: 168 us
  Pallas kernels  153 us (91%)
  local copies, waits for them, and re-layouts  13.6 us (8%)
    pallas_call x1, Pallas kernels, body(): pl.pallas_call(functools.partial(keys_kernel, zs), out_shape=(shape((mode...  67.3 us
    pallas_call x1, Pallas kernels, body(): pl.pallas_call(functools.partial(finish_kernel, zs), out_shape=(shape((to...  65.4 us
    pallas_call x1, Pallas kernels, body(): pl.pallas_call(functools.partial(attention_kernel, zs), out_shape=(jax.Sh...  20.5 us
    unnamed x21, local copies, waits for them, and re-layouts  12.8 us

profile of v2, /device:TPU:1, one launch (start us, length us, event | category | flops | bytes accessed | tf_op | source)
XLA Modules:
  0.0 167.6 jit_solution(14129433488524591754)
XLA Ops:
  0.6 1.1 copy.15.d_ref
  1.7 0.0 copy-start.4
  1.7 1.2 copy-done.4
  2.9 0.0 copy-start.6
  2.9 0.9 copy-done.6
  3.8 0.0 copy-start.7
  3.8 0.7 copy-done.7
  4.6 67.3 %gather_weights_and_keys.1 = (bf16[8192,640]{1,0:T(8,128)(2,1)}, bf16[512,1024]{1,0:T(8,128)(2,1)S(1)}, bf16[512,1024]{1,0:T(8,128)(2,1)S(1)}, bf16[4096,128]{1,...) custom-call(bf16[1024,512]{1,0:T(8,128)(2,1)S(1)} %copy-done.4, ...), custom_call_target="tpu_custom_call" | custom-call | tf_op jit(solution)/shard_map/gather_weights_and_keys/pallas_call | solution.py:802
  71.9 0.0 copy-start
  71.9 1.0 copy-done
  72.9 0.0 copy-start.1
  72.9 1.0 copy-done.1
  73.9 0.0 copy-start.2
  73.9 1.0 copy-done.2
  74.9 0.0 copy-start.3
  74.9 1.0 copy-done.3
  75.9 20.5 %attention_gradients.1 = (bf16[512,1024]{1,0:T(8,128)(2,1)}, bf16[4096,256]{1,0:T(8,128)(2,1)}) custom-call(s32[64]{0:T(128)} %bitcast.29, s32[1,4096]{1,0:T(1,128)} %doc_ref.1, s32[1,4096]{1,0:T(1,128)} %doc_ref.1, bf16[512,1024]{1,0:T(8,128)(2,1)} %copy-done, bf16[512,1024]{1,0:T(8,128)(2,1)} %copy-done.1, bf16[4096,128]{1,0:T(8,128)(2,1)} %copy-done.3, ...), custom_call_target="tpu_custom_call" | custom-call | tf_op jit(solution)/shard_map/attention_gradients/pallas_call | solution.py:838
  96.5 0.0 copy-start.5
  96.5 1.2 copy-done.5
  97.7 65.4 %sum_gradients.1 = (bf16[128,4096]{1,0:T(8,128)(2,1)S(1)}, bf16[128,512]{1,0:T(8,128)(2,1)S(1)}, bf16[128,8192]{1,0:T(8,128)(2,1)S(1)}, f32[2,8,40,128]{3,2,1,0:T(8,128)S(1)}) custom-call(bf16[4096,256]{1,0:T(8,128)(2,1)} %get-tuple-element.22.dkv_ref, bf16[512,1024]{1,0:T(8,128)(2,1)S(1)} %copy-done.5, bf16[128,64]{1,0:T(8,128)(2,1)S(1)} %get-tuple-element.24.low_ref, ...), custom_call_target="tpu_custom_call" | custom-call | tf_op jit(solution)/shard_map/sum_gradients/pallas_call | solution.py:879
  163.1 0.6 slice.7
  163.7 0.2 copy.16
  163.9 0.8 copy.19
  164.6 1.0 copy.23
  165.6 0.7 copy.24
  166.3 1.3 copy.25
  (1 shorter events, 0.0 us)
Async XLA Ops:
  1.7 1.2 copy-start.4
  2.9 0.9 copy-start.6
  3.8 0.7 copy-start.7
  71.9 1.0 copy-start
  72.9 1.0 copy-start.1
  73.9 1.1 copy-start.2
  74.9 1.0 copy-start.3
  96.5 1.2 copy-start.5

commit v3 on v2

--- a/solution.py
+++ b/solution.py
@@ -19,6 +19,7 @@
 MESH = pl.DeviceIdType.MESH
 ANY = pl.BlockSpec(memory_space=pl.ANY)
 VMEM = pl.BlockSpec(memory_space=pltpu.VMEM)
+HBM = pl.BlockSpec(memory_space=pltpu.HBM)
 SMEM = pl.BlockSpec(memory_space=pltpu.SMEM)
 
 
@@ -132,7 +133,7 @@
 
 def keys_kernel(
     zs,
-    w_ref,
+    w_hbm,
     d_ref,
     u_ref,
     x_hbm,
@@ -149,6 +150,7 @@
     full,
     inputs,
     projected,
+    pair_in,
     keys,
     send_sems,
     recv_sems,
@@ -156,15 +158,27 @@
 ):
     place = Place(zs)
     tokens = q_ref.shape[0]
-    shard, kv_width = w_ref.shape
-    rank = d_ref.shape[1]
+    shard, kv_width = w_hbm.shape
+    rank = d_ref.shape[0]
     unit = shard // 8
     width = GROUPS * HEAD_SIZE
     member = place.member
     mine = at((place.z * 4 + member) * tokens, tokens)
     columns = at(member * HEAD_SIZE, HEAD_SIZE)
-    load = pltpu.make_async_copy(x_hbm, inputs, own_sems.at[0])
-    load.start()
+    piece = shard // 2
+
+    def columns_of(f, core):
+        return at(f * shard + core * piece, piece)
+
+    def own_inputs(f):
+        return pltpu.make_async_copy(
+            x_hbm.at[:, columns_of(f, place.core)],
+            inputs.at[:tokens, f * piece : (f + 1) * piece],
+            own_sems.at[0],
+        )
+
+    for f in range(8):
+        own_inputs(f).start()
     owns = [
         pltpu.make_async_copy(
             q_ref.at[:, at(member * width, width)], qg_ref.at[at(member * tokens, tokens)], own_sems.at[1]
@@ -177,10 +191,13 @@
     for own in owns:
         own.start()
     own_rows = at(place.fsdp * shard, shard)
-    full[own_rows, :kv_width] = w_ref[...]
-    up_rows = jnp.concatenate([u_ref[...], jnp.zeros((shard - rank, u_ref.shape[1]), jnp.bfloat16)], axis=0)
-    full[own_rows, kv_width:] = jnp.concatenate([d_ref[...], up_rows], axis=1)
+    weights = pltpu.make_async_copy(w_hbm, full.at[own_rows, :kv_width], own_sems.at[5])
+    weights.start()
+    filler = jnp.zeros((shard // 2 - rank, u_ref.shape[1]), jnp.bfloat16)
+    up_rows = jnp.concatenate([u_ref[...], filler] * 2, axis=0)
+    full[own_rows, kv_width:] = jnp.concatenate([d_ref[...].T, up_rows], axis=1)
     projected[...] = jnp.zeros_like(projected)
+    weights.wait()
 
     right, left, across, sibling = place.at_x(1), place.at_x(3), place.across_y(), place.sibling()
     z_up, z_down = place.at_z(1), place.at_z(-1)
@@ -194,32 +211,85 @@
         begin = f * shard + place.core * 4 * unit + offset
         return full.at[pl.ds(pl.multiple_of(begin, unit // 2), size)]
 
-    def main(f):
-        return rows_of(f, parity * unit, 3 * unit)
+    def bridge(f):
+        return rows_of(f, parity * 3 * unit, unit)
+
+    def body(f):
+        return rows_of(f, unit, 2 * unit)
+
+    def low_body(f):
+        return rows_of(f, unit, unit // 2)
+
+    def high_body(f):
+        return rows_of(f, unit + unit // 2, 3 * unit // 2)
 
     def pass_on(block, *devices):
         return [send(block, block, device) for device in devices]
-
-    half = 3 * unit // 2
-
-    def first_half(f):
-        return rows_of(f, parity * unit, half)
-
-    def second_half(f):
-        return rows_of(f, parity * unit + half, half)
 
     y_hi, x = place.y_hi, place.x
     row = lambda y, step: place.row(y, x + step)
     own, near_left, near_right, far = (row(y_hi, k) for k in (0, 3, 1, 2))
     over, over_left, over_right, over_far = (row(1 - y_hi, k) for k in (0, 3, 1, 2))
 
+    sibling_inputs = [
+        send(
+            x_hbm.at[:, columns_of(f, 1 - place.core)],
+            inputs.at[tokens:, f * piece : (f + 1) * piece],
+            sibling,
+        )
+        for f in range(8)
+    ]
     value_copies = [
         send(
             v_ref.at[:, at(place.fellow(k) * HEAD_SIZE, HEAD_SIZE)], vg_ref.at[mine], place.at_fellow(k)
         )
         for k in (1, 2, 3)
     ]
-    from_left, from_right, from_over = pass_on(main(own), right, left, across)
+    near_left_bridge, near_right_bridge, over_bridge = pass_on(bridge(own), right, left, across)
+    near_left_body, near_right_body, over_body = pass_on(body(own), right, left, across)
+    shares = {}
+    crossing = {}
+
+    def share(name, f):
+        shares[name] = pass_on(rows_of(f, parity * unit, 3 * unit), sibling)[0]
+
+    def cross(name, f):
+        begin = parity * 3 * unit
+        crossing[name] = (
+            pass_on(rows_of(f, begin, unit // 2), z_up)
+            + pass_on(rows_of(f, begin + unit // 2, unit // 2), z_down)
+        )
+
+    def land(name, f):
+        for copy in crossing[name]:
+            copy.wait_recv()
+        shares[name, "rest"] = pass_on(rows_of(f, (1 - parity) * 3 * unit, unit), sibling)[0]
+
+    def multiply(f, offset, size):
+        columns = pl.ds(pl.multiple_of(f * piece + offset, unit), size)
+        projected[...] += jnp.dot(
+            inputs[:, columns], rows_of(f, offset, size)[...], preferred_element_type=jnp.float32
+        )
+
+    def project(f):
+        multiply(f, parity * unit, 3 * unit)
+
+    def project_rest(f):
+        multiply(f, (1 - parity) * 3 * unit, unit)
+
+    pltpu.make_async_copy(x_hbm.at[:, : 8 * piece], inputs.at[:tokens], own_sems.at[0]).wait()
+    for copy in sibling_inputs:
+        copy.wait_recv()
+    multiply(own, 0, 4 * unit)
+
+    near_left_bridge.wait_recv()
+    far_bridge = pass_on(bridge(near_left), right)[0]
+    cross("near_left", near_left)
+    near_right_bridge.wait_recv()
+    cross("near_right", near_right)
+    over_bridge.wait_recv()
+    over_left_bridge, over_right_bridge = pass_on(bridge(over), right, left)
+    cross("over", over)
     head_copies = []
     for k in (2, 3, 1):
         for src, dst in ((q_ref, qg_ref), (g_ref, gg_ref)):
@@ -231,93 +301,71 @@
                 )
             )
 
-    shares = {}
-    crossing = {}
-
-    def share(name, block):
-        shares.setdefault(name, []).extend(pass_on(block, sibling))
-
-    def cross(name, f):
-        bridge = parity * 3 * unit
-        crossing[name] = (
-            pass_on(rows_of(f, bridge, unit // 2), z_up)
-            + pass_on(rows_of(f, bridge + unit // 2, unit // 2), z_down)
-        )
-
-    def land(name, f):
-        for copy in crossing[name]:
-            copy.wait_recv()
-        share(name, rows_of(f, (1 - parity) * 3 * unit, unit))
-
-    def project(name, f):
-        for copy in shares.get(name, ()):
-            copy.wait_recv()
-
-        @pl.loop(0, 2)
-        def _(part):
-            rows = at(f * shard + part * (shard // 2), shard // 2)
-            projected[...] += jnp.dot(inputs[:, rows], full[rows, :], preferred_element_type=jnp.float32)
-
-    load.wait()
-    project("own", own)
+    near_left_body.wait_recv()
+    far_low = pass_on(low_body(near_left), right)[0]
+    near_right_body.wait_recv()
+    far_high = pass_on(high_body(near_right), left)[0]
+    over_body.wait_recv()
+    over_left_body, over_right_body = pass_on(body(over), right, left)
+    share("near_left", near_left)
+    share("near_right", near_right)
+    share("over", over)
+    far_bridge.wait_recv()
+    over_far_bridge = pass_on(bridge(far), across)[0]
+    cross("far", far)
+    far_low.wait_recv()
+    over_far_low = pass_on(low_body(far), across)[0]
+    for name, f in (("near_left", near_left), ("near_right", near_right), ("over", over)):
+        land(name, f)
+    far_high.wait_recv()
+    over_far_high = pass_on(high_body(far), across)[0]
+    share("far", far)
     for copy in value_copies:
         copy.wait_recv()
     owns[2].wait()
     ring = Ring(place, sender, vg_ref, lambda z: z * 4 * tokens, 4 * tokens)
-    ring.step()
-
-    from_left.wait_recv()
-    far_first = pass_on(first_half(near_left), right)[0]
-    from_right.wait_recv()
-    far_second = pass_on(second_half(near_right), left)[0]
-    from_over.wait_recv()
-    over_from_left, over_from_right = pass_on(main(over), right, left)
-    for name, f in (("near_left", near_left), ("near_right", near_right), ("over", over)):
-        share(name, main(f))
-        cross(name, f)
-    ring.step()
-    far_first.wait_recv()
-    over_far_first = pass_on(first_half(far), across)[0]
-    far_second.wait_recv()
-    over_far_second = pass_on(second_half(far), across)[0]
-    share("far", main(far))
-    cross("far", far)
-    ring.step()
-    for name, f in (("near_left", near_left), ("near_right", near_right), ("over", over)):
+    over_left_bridge.wait_recv()
+    cross("over_left", over_left)
+    over_right_bridge.wait_recv()
+    cross("over_right", over_right)
+    over_far_bridge.wait_recv()
+    cross("over_far", over_far)
+    land("far", far)
+    for f in (near_left, near_right, over, far):
+        project(f)
+        project_rest(f)
+    over_left_body.wait_recv()
+    project(over_left)
+    share("over_left", over_left)
+    over_right_body.wait_recv()
+    project(over_right)
+    share("over_right", over_right)
+    for name, f in (("over_left", over_left), ("over_right", over_right), ("over_far", over_far)):
         land(name, f)
-    project("near_left", near_left)
-    project("near_right", near_right)
-    land("far", far)
-    ring.run()
-    project("over", over)
-    over_from_left.wait_recv()
-    share("over_left", main(over_left))
-    cross("over_left", over_left)
-    over_from_right.wait_recv()
-    share("over_right", main(over_right))
-    cross("over_right", over_right)
-    project("far", far)
-    over_far_first.wait_recv()
-    over_far_second.wait_recv()
-    share("over_far", main(over_far))
-    cross("over_far", over_far)
-    land("over_left", over_left)
-    land("over_right", over_right)
-    project("over_left", over_left)
-    project("over_right", over_right)
-    land("over_far", over_far)
-    project("over_far", over_far)
-    store = pltpu.make_async_copy(full, full_ref, own_sems.at[0])
-    store.start()
-
-    low_rank = projected[:, kv_width : kv_width + rank].astype(jnp.bfloat16)
+        project_rest(f)
+    over_far_low.wait_recv()
+    over_far_high.wait_recv()
+    project(over_far)
+    pair_copy = send(projected.at[tokens:], pair_in, sibling)
+    share("over_far", over_far)
+
+    def stores(core):
+        for f in range(8):
+            rows = columns_of(f, core)
+            pltpu.make_async_copy(full.at[rows], full_ref.at[rows], own_sems.at[0]).start()
+
+    stores(place.core)
+    pair_copy.wait_recv()
+    projection = projected[:tokens] + pair_in[...]
+
+    low_rank = projection[:, kv_width : kv_width + rank].astype(jnp.bfloat16)
     low_ref[...] = low_rank
     for f in range(8):
         up_ref[:, f * (kv_width // 8) : (f + 1) * (kv_width // 8)] = full[
-            f * shard : f * shard + rank, kv_width + rank :
+            at(f * shard + place.core * piece, rank), kv_width + rank :
         ]
     keys[...] = (
-        projected[:, :kv_width]
+        projection[:, :kv_width]
         + ADAPTER_SCALE * jnp.dot(low_rank, up_ref[...], preferred_element_type=jnp.float32)
     ).astype(jnp.bfloat16)
     own_keys = pltpu.make_async_copy(keys.at[:, columns], kg_ref.at[mine], own_sems.at[4])
@@ -342,15 +390,20 @@
     for copy in other:
         copy.wait_recv()
     rings[1].step()
-    while any(ring.flying for ring in rings):
-        for ring in rings:
-            ring.step()
+    for copy in shares.values():
+        copy.wait_recv()
+    stores(1 - place.core)
+    rings.append(ring)
+    ring.step()
+    while any(some.flying for some in rings):
+        for some in rings:
+            some.step()
     for copy in head_copies:
         copy.wait_recv()
     sender.finish()
     owns[0].wait()
     owns[1].wait()
-    store.wait()
+    pltpu.make_async_copy(full, full_ref, own_sems.at[0]).wait()
 
 
 def attention_kernel(
@@ -358,25 +411,21 @@
     list_ref,
     doc_smem,
     doc_ref,
-    q_hbm,
-    g_hbm,
-    k_hbm,
-    v_hbm,
-    dq_hbm,
-    dkv_hbm,
     queries,
     gradients,
+    k_ref,
+    v_ref,
+    dq_hbm,
+    dkv_ref,
     keys,
     values,
     totals,
     scores,
     grads,
     dq_rows,
-    rounded,
     firsts,
     starts,
-    load_sems,
-    store_sems,
+    store_sem,
 ):
     to_exponent = math.log2(math.e) / math.sqrt(HEAD_SIZE)
     inv_root = 1.0 / math.sqrt(HEAD_SIZE)
@@ -385,25 +434,6 @@
     own_spans = queries.shape[0] // SPAN
     z = lax.div(lax.axis_index("context"), 4)
     length = spans * SPAN
-
-    loads = [
-        pltpu.make_async_copy(q_hbm, queries, load_sems.at[0]),
-        pltpu.make_async_copy(g_hbm, gradients, load_sems.at[1]),
-    ]
-    for load in loads:
-        load.start()
-
-    def span_copies(s):
-        src, dst = at(s * SPAN, SPAN), at(list_ref[s] * SPAN, SPAN)
-        return (
-            pltpu.make_async_copy(k_hbm.at[src], keys.at[dst], load_sems.at[2]),
-            pltpu.make_async_copy(v_hbm.at[src], values.at[dst], load_sems.at[3]),
-        )
-
-    @pl.loop(0, spans)
-    def _(s):
-        for load in span_copies(s):
-            load.start()
 
     keys[length:, :] = jnp.zeros((KEY_TILE, HEAD_SIZE), jnp.bfloat16)
     values[length:, :] = jnp.zeros((KEY_TILE, HEAD_SIZE), jnp.bfloat16)
@@ -440,11 +470,11 @@
         changes = jnp.maximum(changes, jnp.where(lane >= step, pltpu.roll(changes, step, 1), 0))
     starts[...] = jnp.where(changes == 0, row_first, row_begin + changes)
 
-    for load in loads:
-        load.wait()
-
-    pltpu.make_async_copy(k_hbm, keys.at[:length], load_sems.at[2]).wait()
-    pltpu.make_async_copy(v_hbm, values.at[:length], load_sems.at[3]).wait()
+    @pl.loop(0, spans)
+    def _(s):
+        src, dst = at(s * SPAN, SPAN), at(list_ref[s] * SPAN, SPAN)
+        keys[dst, :] = k_ref[src, :]
+        values[dst, :] = v_ref[src, :]
 
     @pl.loop(0, own_spans)
     def _(i):
@@ -511,16 +541,13 @@
         dq = dq.T.astype(jnp.bfloat16)
         for g in range(GROUPS):
             dq_rows[own, g * HEAD_SIZE : (g + 1) * HEAD_SIZE] = dq[g * SPAN : (g + 1) * SPAN]
-        pltpu.make_async_copy(dq_rows.at[own], dq_hbm.at[own], store_sems.at[0]).start()
+        pltpu.make_async_copy(dq_rows.at[own], dq_hbm.at[own], store_sem).start()
 
     @pl.loop(0, spans)
     def _(s):
-        rows = at(s * SPAN, SPAN)
-        rounded[rows, :] = totals[at(list_ref[s] * SPAN, SPAN), :].astype(jnp.bfloat16)
-        pltpu.make_async_copy(rounded.at[rows], dkv_hbm.at[rows], store_sems.at[1]).start()
-
-    pltpu.make_async_copy(dq_rows, dq_hbm, store_sems.at[0]).wait()
-    pltpu.make_async_copy(rounded, dkv_hbm, store_sems.at[1]).wait()
+        dkv_ref[at(s * SPAN, SPAN), :] = totals[at(list_ref[s] * SPAN, SPAN), :].astype(jnp.bfloat16)
+
+    pltpu.make_async_copy(dq_rows, dq_hbm, store_sem).wait()
 
 
 REDUCE_CUTS = 2
@@ -542,6 +569,8 @@
     dq_ref,
     vg_ref,
     grad_ref,
+    down_ref,
+    up_out,
     total_ref,
     out,
     held,
@@ -756,6 +785,14 @@
         copy.wait_recv()
     block = total_ref.at[place.core]
     send(block, block, sibling).wait_recv()
+    for core in range(2):
+        for j in range(zs):
+            down_ref[core * ranks : (core + 1) * ranks, j * chunk_lanes : (j + 1) * chunk_lanes] = total_ref[
+                core, j, :ranks
+            ]
+        for j in range(cuts):
+            begin = core * ranks + j * small
+            up_out[begin : begin + small, :] = total_ref[core, j, ranks:, :share]
     for copy in value_copies + query_copies:
         copy.wait_recv()
     sender.finish()
@@ -767,11 +804,11 @@
     return pltpu.SemaphoreType.DMA((count,))
 
 
-def params(collective_id=None):
+def params(mebibytes, collective_id=None):
     if collective_id is None:
-        return pltpu.CompilerParams(vmem_limit_bytes=56 << 20)
+        return pltpu.CompilerParams(vmem_limit_bytes=mebibytes << 20)
     return pltpu.CompilerParams(
-        vmem_limit_bytes=48 << 20, collective_id=collective_id, has_side_effects=True
+        vmem_limit_bytes=mebibytes << 20, collective_id=collective_id, has_side_effects=True
     )
 
 
@@ -798,7 +835,7 @@
     shape = jax.ShapeDtypeStruct
     packed_width = kv_width + rank + adapter_up.shape[1]
 
-    copies = 3 + 3 + 6 + 2 + 2 + 2 + 7 * 4 + 3 + 3 * 2 * half
+    copies = 9 + 3 + 6 + 6 + 3 + 4 + 3 + 7 * 4 + 3 + 3 * 2 * half
     full, query_group, gradient_group, value_all, key_all, low_rank, complete_up = pl.pallas_call(
         functools.partial(keys_kernel, zs),
         out_shape=(
@@ -810,22 +847,23 @@
             shape((tokens, rank), bf16),
             shape((rank, kv_width), bf16),
         ),
-        in_specs=[VMEM] * 3 + [ANY] * 4,
-        out_specs=(ANY,) * 5 + (VMEM,) * 2,
+        in_specs=[ANY, VMEM, VMEM, ANY, ANY, ANY, ANY],
+        out_specs=(ANY,) + (VMEM,) * 6,
         scratch_shapes=[
             pltpu.VMEM((model, packed_width), bf16),
-            pltpu.VMEM((tokens, model), bf16),
+            pltpu.VMEM((2 * tokens, model // 2), bf16),
+            pltpu.VMEM((2 * tokens, packed_width), f32),
             pltpu.VMEM((tokens, packed_width), f32),
             pltpu.VMEM((tokens, kv_width), bf16),
             dma(copies),
             dma(copies),
-            dma(5),
+            dma(6),
         ],
-        compiler_params=params(0),
+        compiler_params=params(48, 0),
         name="gather_weights_and_keys",
     )(
         key_base_weight,
-        adapter_down,
+        adapter_down.T,
         adapter_up,
         rows_in,
         queries[0],
@@ -841,24 +879,20 @@
             jax.ShapeDtypeStruct((span_rows, width), bf16),
             jax.ShapeDtypeStruct((length, 2 * HEAD_SIZE), bf16),
         ),
-        in_specs=[SMEM, SMEM, VMEM] + [ANY] * 4,
-        out_specs=(ANY, ANY),
+        in_specs=[SMEM, SMEM] + [VMEM] * 5,
+        out_specs=(ANY, VMEM),
         scratch_shapes=[
-            pltpu.VMEM((span_rows, width), bf16),
-            pltpu.VMEM((span_rows, width), bf16),
             pltpu.VMEM((length + KEY_TILE, HEAD_SIZE), bf16),
             pltpu.VMEM((length + KEY_TILE, HEAD_SIZE), bf16),
             pltpu.VMEM((length + KEY_TILE, 2 * HEAD_SIZE), f32),
             pltpu.VMEM(tile_rows, f32),
             pltpu.VMEM(tile_rows, f32),
             pltpu.VMEM((span_rows, width), bf16),
-            pltpu.VMEM((length, 2 * HEAD_SIZE), bf16),
             pltpu.SMEM((span_rows // SPAN,), i32),
             pltpu.VMEM((span_rows // SPAN, 2 * SPAN), i32),
-            dma(4),
-            dma(2),
+            pltpu.SemaphoreType.DMA,
         ],
-        compiler_params=params(),
+        compiler_params=params(24),
         name="attention_gradients",
     )(
         span_slot_index[0],
@@ -876,17 +910,19 @@
     lanes = shard + 128
     chunk = (ranks + ranks // min(zs, 4), shard // zs)
     copies = hops + 9 + 1 + 6 + 1 + 2 * (zs - 1) + 2
-    query_grad, value_grad, input_gradient, totals = pl.pallas_call(
+    query_grad, value_grad, input_gradient, down_share, up_share = pl.pallas_call(
         functools.partial(finish_kernel, zs),
         out_shape=(
             shape((tokens, QUERY_HEADS * HEAD_SIZE), bf16),
             shape((tokens, kv_width), bf16),
             shape((tokens, model), bf16),
-            shape((2, zs) + chunk, f32),
+            shape((rank, shard), f32),
+            shape((rank, adapter_up.shape[1]), f32),
         ),
-        in_specs=[VMEM, ANY, VMEM, VMEM, ANY, ANY],
-        out_specs=(ANY, ANY, VMEM, VMEM),
+        in_specs=[VMEM, ANY, VMEM, VMEM, HBM, HBM],
+        out_specs=(ANY, ANY, VMEM, VMEM, VMEM),
         scratch_shapes=[
+            pltpu.VMEM((2, zs) + chunk, f32),
             pltpu.VMEM((hops, cut, HEAD_SIZE), bf16),
             pltpu.VMEM((hops, cut, HEAD_SIZE), bf16),
             pltpu.VMEM((2, 4 * tokens, HEAD_SIZE), bf16),
@@ -910,14 +946,11 @@
             dma(copies),
             dma(5),
         ],
-        compiler_params=params(1),
+        compiler_params=params(44, 1),
         name="sum_gradients",
     )(partial_sums, query_grad_group, low_rank, complete_up, rows_in, full)
 
-    share = kv_width // 8
-    down_share = totals[:, :, :ranks].transpose(1, 3, 0, 2).reshape(shard, rank)
-    up_share = totals[:, : min(zs, 4), ranks:, :share].reshape(rank, share)
-    return (query_grad[None], value_grad[None], input_gradient[None], down_share, up_share)
+    return (query_grad[None], value_grad[None], input_gradient[None], down_share.T, up_share)
 
 
 def solution(mesh):

time: 168 us -> 158 us (0.940)
  local copies, waits for them, and re-layouts: 13.6 us -> 8.02 us
  Pallas kernels: 153 us -> 149 us
    unnamed x21 -> x19, local copies, waits for them, and re-layouts: 12.8 us -> 8.02 us
    pallas_call x1, Pallas kernels: 20.5 us -> 17.1 us  [body(): pl.pallas_call(functools.partial(attention_kernel, zs), out_shape=(jax.Sh...]
where the time goes in v3:
time: 158 us
  Pallas kernels  149 us (94%)
  local copies, waits for them, and re-layouts  8.02 us (5%)
    pallas_call x1, Pallas kernels, body(): pl.pallas_call(functools.partial(keys_kernel, zs), out_shape=(shape((mode...  66.2 us
    pallas_call x1, Pallas kernels, body(): pl.pallas_call(functools.partial(finish_kernel, zs), out_shape=(shape((to...  65.8 us
    pallas_call x1, Pallas kernels, body(): pl.pallas_call(functools.partial(attention_kernel, zs), out_shape=(jax.Sh...  17.1 us
    unnamed x19, local copies, waits for them, and re-layouts  8.02 us

profile of v3, /device:TPU:1, one launch (start us, length us, event | category | flops | bytes accessed | tf_op | source)
XLA Modules:
  0.0 157.8 jit_solution(10339063223776563539)
XLA Ops:
  0.6 0.0 copy-start.1
  0.6 1.2 copy-done.1
  1.9 0.0 copy-start.2
  1.9 0.9 copy-done.2
  2.8 0.0 copy-start.3
  2.8 0.9 copy-done.3
  3.7 0.0 copy-start.5
  3.7 0.7 copy-done.5
  4.4 0.0 copy-start.4
  4.4 0.0 copy-start.6
  4.4 66.2 %gather_weights_and_keys.1 = (bf16[8192,640]{1,0:T(8,128)(2,1)}, bf16[512,1024]{1,0:T(8,128)(2,1)S(1)}, bf16[512,1024]{1,0:T(8,128)(2,1)S(1)}, bf16[4096,128]{1,...) custom-call(bf16[1024,512]{1,0:T(8,128)(2,1)S(1)} %copy-done.1, ...), custom_call_target="tpu_custom_call" | custom-call | tf_op jit(solution)/shard_map/gather_weights_and_keys/pallas_call | solution.py:839
  70.6 0.0 copy-done.4
  70.6 0.0 copy-done.6
  70.6 0.0 copy-start
  70.6 17.1 %attention_gradients.1 = (bf16[512,1024]{1,0:T(8,128)(2,1)S(1)}, bf16[4096,256]{1,0:T(8,128)(2,1)S(1)}) custom-call(s32[64]{0:T(128)S(1)} %bitcast.18, s32[1,4096]{1,0:T(1,128)S(1)} %copy-done.4, s32[1,4096]{1,0:T(1,128)S(1)} %copy-done.4, bf16[512,1024]{1,0:T(8,128)(2,1)S(1)} %get-tuple-element.19.queries, ...), custom_call_target="tpu_custom_call" | custom-call | tf_op jit(solution)/shard_map/attention_gradients/pallas_call | solution.py:876
  87.7 0.0 copy-done
  87.7 65.8 %sum_gradients.1 = (bf16[128,4096]{1,0:T(8,128)(2,1)S(1)}, bf16[128,512]{1,0:T(8,128)(2,1)S(1)}, bf16[128,8192]{1,0:T(8,128)(2,1)S(1)}, f32[64,1024]{1,0:T(8,128)S(1)}, f32[64,64]{1,0:T(8,128)S(1)}) custom-call(bf16[4096,256]{1,0:T(8,128)(2,1)S(1)} %get-tuple-element.23.dkv_ref, bf16[512,1024]{1,0:T(8,128)(2,1)S(1)} %get-tuple-element.24.dqg_ref, ...), custom_call_target="tpu_custom_call" | custom-call | tf_op jit(solution)/shard_map/sum_gradients/pallas_call | solution.py:913
  153.5 1.0 copy.19
  154.5 0.7 copy.20
  155.1 1.3 copy.21
  156.5 0.7 copy.22
  157.2 0.6 copy.23
Async XLA Ops:
  0.6 1.2 copy-start.1
  1.9 0.9 copy-start.2
  2.8 0.9 copy-start.3
  3.7 0.7 copy-start.5
  4.4 66.2 %copy-start.4 = (s32[1,4096]{1,0:T(1,128)S(1)}, s32[1,4096]{1,0:T(1,128)}, u32[]{:S(2)}) copy-start(s32[1,4096]{1,0:T(1,128)} %doc_ref.1) | copy-start | bytes 49156
  4.4 66.2 %copy-start.6 = (s32[1,64]{1,0:T(1,128)S(1)}, s32[1,64]{1,0:T(1,128)}, u32[]{:S(2)}) copy-start(s32[1,64]{1,0:T(1,128)} %param.16) | copy-start | bytes 772
  70.6 17.2 %copy-start = (bf16[1,128,8192]{2,1,0:T(8,128)(2,1)S(1)}, bf16[1,128,8192]{2,1,0:T(8,128)(2,1)}, u32[]{:S(2)}) copy-start(bf16[1,128,8192]{2,1,0:T(8,128)(2,1)} %param.9) | copy-start | bytes 6291460

commit v4 on v3

--- a/solution.py
+++ b/solution.py
@@ -324,6 +324,7 @@
         copy.wait_recv()
     owns[2].wait()
     ring = Ring(place, sender, vg_ref, lambda z: z * 4 * tokens, 4 * tokens)
+    ring.step()
     over_left_bridge.wait_recv()
     cross("over_left", over_left)
     over_right_bridge.wait_recv()
@@ -340,6 +341,7 @@
     over_right_body.wait_recv()
     project(over_right)
     share("over_right", over_right)
+    ring.step()
     for name, f in (("over_left", over_left), ("over_right", over_right), ("over_far", over_far)):
         land(name, f)
         project_rest(f)
@@ -355,6 +357,7 @@
             pltpu.make_async_copy(full.at[rows], full_ref.at[rows], own_sems.at[0]).start()
 
     stores(place.core)
+    ring.step()
     pair_copy.wait_recv()
     projection = projected[:tokens] + pair_in[...]
 
@@ -423,6 +426,8 @@
     scores,
     grads,
     dq_rows,
+    q_columns,
+    g_columns,
     firsts,
     starts,
     store_sem,
@@ -488,6 +493,8 @@
         )
         pair = starts[pl.ds(i, 1), :]
         own_start = jnp.where(lax.rem(slot, 2) == 1, pair[:, SPAN:], pair[:, :SPAN])
+        q_columns[...] = q_rows.T
+        g_columns[...] = g_rows.T
         q_start = jnp.concatenate([own_start] * GROUPS, axis=1) - first * SPAN
         lane = lax.broadcasted_iota(jnp.int32, (1, lanes), 1)
         q_pos = (slot - first) * SPAN + lax.rem(lane, SPAN)
@@ -497,17 +504,13 @@
             return pl.ds(pl.multiple_of(first * SPAN + t * KEY_TILE, SPAN), KEY_TILE)
 
         def peak_step(t, peak, q_rows=q_rows, q_start=q_start, q_pos=q_pos, rows_at=rows_at):
-            raw = lax.dot_general(
-                keys[rows_at(t), :], q_rows, (((1,), (1,)), ((), ())), preferred_element_type=jnp.float32
-            )
+            raw = jnp.dot(keys[rows_at(t), :], q_columns[...], preferred_element_type=jnp.float32)
             key_pos = lax.broadcasted_iota(jnp.int32, (KEY_TILE, lanes), 0)
             raw = jnp.where(
                 (key_pos >= q_start - t * KEY_TILE) & (key_pos <= q_pos - t * KEY_TILE), raw, NEGATIVE_FILL
             )
             scores[t] = raw
-            grads[t] = lax.dot_general(
-                values[rows_at(t), :], g_rows, (((1,), (1,)), ((), ())), preferred_element_type=jnp.float32
-            )
+            grads[t] = jnp.dot(values[rows_at(t), :], g_columns[...], preferred_element_type=jnp.float32)
             return jnp.maximum(peak, jnp.max(raw, axis=0, keepdims=True))
 
         peak = lax.fori_loop(0, tiles, peak_step, jnp.full((1, lanes), NEGATIVE_FILL, jnp.float32))
@@ -589,8 +592,6 @@
     y_in,
     z_out,
     z_in,
-    lo_out,
-    lo_in,
     send_sems,
     recv_sems,
     own_sems,
@@ -613,10 +614,11 @@
     own_query.start()
     right, left, across = place.at_x(1), place.at_x(3), place.across_y()
     sibling, other_lo = place.sibling(), place.other_y_lo()
+    beyond = {"fsdp": place.row(1 - place.y_hi, place.x), "context": place.context}
     greet(
         [place.at_fellow(k) for k in (1, 2, 3)]
         + [place.at_z(k) for k in range(1, zs)]
-        + [right, left, across]
+        + [right, left, across, beyond]
     )
     sender = Sender(send_sems, recv_sems)
     send = sender.send
@@ -750,12 +752,15 @@
     def over_x(y_hi):
         return add(row[here(y_hi, 0)], near_in[0, y_hi], near_in[1, y_hi])
 
-    y_out[...] = over_x(1 - place.y_hi).astype(jnp.bfloat16)
-    y_copy = send(y_out, y_in, across)
+    y_out[0] = over_x(1 - place.y_hi).astype(jnp.bfloat16)
+    y_copies = [send(y_out.at[0], y_in.at[0], beyond), send(y_out.at[0], y_in.at[1], across)]
     mine = over_x(place.y_hi)
+    y_out[1] = mine.astype(jnp.bfloat16)
+    y_copies.append(send(y_out.at[1], y_in.at[2], other_lo))
     input_gradient(5, 6)
-    y_copy.wait_recv()
-    mine = add(mine, y_in[...])
+    for copy in y_copies:
+        copy.wait_recv()
+    mine = add(mine, y_in[0], y_in[1], y_in[2])
     chunk_lanes = lanes // zs
     cuts = min(zs, 4)
     small = ranks // cuts
@@ -771,10 +776,6 @@
     chunk = z_out[place.z]
     for k in range(zs - 1):
         chunk = chunk + z_in[k]
-    lo_out[...] = chunk
-    lo_copy = send(lo_out, lo_in, other_lo)
-    lo_copy.wait_recv()
-    chunk = chunk + lo_in[...]
     total_ref[pl.ds(place.core, 1), pl.ds(place.z, 1)] = chunk[None, None]
     block = total_ref.at[place.core, place.z]
     z_copies = []
@@ -888,6 +889,8 @@
             pltpu.VMEM(tile_rows, f32),
             pltpu.VMEM(tile_rows, f32),
             pltpu.VMEM((span_rows, width), bf16),
+            pltpu.VMEM((HEAD_SIZE, GROUPS * SPAN), bf16),
+            pltpu.VMEM((HEAD_SIZE, GROUPS * SPAN), bf16),
             pltpu.SMEM((span_rows // SPAN,), i32),
             pltpu.VMEM((span_rows // SPAN, 2 * SPAN), i32),
             pltpu.SemaphoreType.DMA,
@@ -909,7 +912,7 @@
     ranks = rank // 2
     lanes = shard + 128
     chunk = (ranks + ranks // min(zs, 4), shard // zs)
-    copies = hops + 9 + 1 + 6 + 1 + 2 * (zs - 1) + 2
+    copies = hops + 9 + 1 + 6 + 3 + 2 * (zs - 1) + 1
     query_grad, value_grad, input_gradient, down_share, up_share = pl.pallas_call(
         functools.partial(finish_kernel, zs),
         out_shape=(
@@ -936,12 +939,10 @@
             pltpu.VMEM((2, ranks, lanes), bf16),
             pltpu.VMEM((2, ranks, lanes), bf16),
             pltpu.VMEM((2, 2, ranks, lanes), bf16),
-            pltpu.VMEM((ranks, lanes), bf16),
-            pltpu.VMEM((ranks, lanes), bf16),
+            pltpu.VMEM((2, ranks, lanes), bf16),
+            pltpu.VMEM((3, ranks, lanes), bf16),
             pltpu.VMEM((zs,) + chunk, f32),
             pltpu.VMEM((zs - 1,) + chunk, f32),
-            pltpu.VMEM(chunk, f32),
-            pltpu.VMEM(chunk, f32),
             dma(copies),
             dma(copies),
             dma(5),

time: 158 us -> 155 us (0.981); the launches traced: 158 us -> 153 us
  Pallas kernels: 149 us -> 144 us
    pallas_call x1, Pallas kernels: 66.2 us -> 61.3 us  [body(): pl.pallas_call(functools.partial(keys_kernel, zs), out_shape=(shape((mode...]
where the time goes in v4:
time: 155 us; the launch traced here: 153 us
  Pallas kernels  144 us (93%)
  local copies, waits for them, and re-layouts  8.02 us (5%)
    pallas_call x1, Pallas kernels, body(): pl.pallas_call(functools.partial(finish_kernel, zs), out_shape=(shape((to...  66.8 us
    pallas_call x1, Pallas kernels, body(): pl.pallas_call(functools.partial(keys_kernel, zs), out_shape=(shape((mode...  61.3 us
    pallas_call x1, Pallas kernels, body(): pl.pallas_call(functools.partial(attention_kernel, zs), out_shape=(jax.Sh...  16.3 us
    unnamed x19, local copies, waits for them, and re-layouts  8.02 us

profile of v4, /device:TPU:1, one launch (start us, length us, event | category | flops | bytes accessed | tf_op | source)
XLA Modules:
  0.0 153.2 jit_solution(11785207021061697583)
XLA Ops:
  0.6 0.0 copy-start.1
  0.6 1.2 copy-done.1
  1.9 0.0 copy-start.2
  1.9 0.9 copy-done.2
  2.8 0.0 copy-start.3
  2.8 0.9 copy-done.3
  3.7 0.0 copy-start.5
  3.7 0.7 copy-done.5
  4.4 0.0 copy-start.4
  4.4 0.0 copy-start.6
  4.4 61.3 %gather_weights_and_keys.1 = (bf16[8192,640]{1,0:T(8,128)(2,1)}, bf16[512,1024]{1,0:T(8,128)(2,1)S(1)}, bf16[512,1024]{1,0:T(8,128)(2,1)S(1)}, bf16[4096,128]{1,...) custom-call(bf16[1024,512]{1,0:T(8,128)(2,1)S(1)} %copy-done.1, ...), custom_call_target="tpu_custom_call" | custom-call | tf_op jit(solution)/shard_map/gather_weights_and_keys/pallas_call | solution.py:840
  65.7 0.0 copy-done.4
  65.7 0.0 copy-done.6
  65.8 0.0 copy-start
  65.8 16.3 %attention_gradients.1 = (bf16[512,1024]{1,0:T(8,128)(2,1)S(1)}, bf16[4096,256]{1,0:T(8,128)(2,1)S(1)}) custom-call(s32[64]{0:T(128)S(1)} %bitcast.18, s32[1,4096]{1,0:T(1,128)S(1)} %copy-done.4, s32[1,4096]{1,0:T(1,128)S(1)} %copy-done.4, bf16[512,1024]{1,0:T(8,128)(2,1)S(1)} %get-tuple-element.19.queries, ...), custom_call_target="tpu_custom_call" | custom-call | tf_op jit(solution)/shard_map/attention_gradients/pallas_call | solution.py:877
  82.0 0.0 copy-done
  82.0 66.8 %sum_gradients.1 = (bf16[128,4096]{1,0:T(8,128)(2,1)S(1)}, bf16[128,512]{1,0:T(8,128)(2,1)S(1)}, bf16[128,8192]{1,0:T(8,128)(2,1)S(1)}, f32[64,1024]{1,0:T(8,128)S(1)}, f32[64,64]{1,0:T(8,128)S(1)}) custom-call(bf16[4096,256]{1,0:T(8,128)(2,1)S(1)} %get-tuple-element.23.dkv_ref, bf16[512,1024]{1,0:T(8,128)(2,1)S(1)} %get-tuple-element.24.dqg_ref, ...), custom_call_target="tpu_custom_call" | custom-call | tf_op jit(solution)/shard_map/sum_gradients/pallas_call | solution.py:916
  148.9 1.0 copy.19
  149.9 0.7 copy.20
  150.5 1.3 copy.21
  151.8 0.7 copy.22
  152.5 0.6 copy.23
Async XLA Ops:
  0.6 1.2 copy-start.1
  1.9 0.9 copy-start.2
  2.8 0.9 copy-start.3
  3.7 0.7 copy-start.5
  4.4 61.4 %copy-start.4 = (s32[1,4096]{1,0:T(1,128)S(1)}, s32[1,4096]{1,0:T(1,128)}, u32[]{:S(2)}) copy-start(s32[1,4096]{1,0:T(1,128)} %doc_ref.1) | copy-start | bytes 49156
  4.4 61.4 %copy-start.6 = (s32[1,64]{1,0:T(1,128)S(1)}, s32[1,64]{1,0:T(1,128)}, u32[]{:S(2)}) copy-start(s32[1,64]{1,0:T(1,128)} %param.16) | copy-start | bytes 772
  65.8 16.3 %copy-start = (bf16[1,128,8192]{2,1,0:T(8,128)(2,1)S(1)}, bf16[1,128,8192]{2,1,0:T(8,128)(2,1)}, u32[]{:S(2)}) copy-start(bf16[1,128,8192]{2,1,0:T(8,128)(2,1)} %param.9) | copy-start | bytes 6291460

commit v5 on v4

--- a/solution.py
+++ b/solution.py
@@ -393,11 +393,13 @@
     for copy in other:
         copy.wait_recv()
     rings[1].step()
-    for copy in shares.values():
-        copy.wait_recv()
-    stores(1 - place.core)
     rings.append(ring)
     ring.step()
+    for some in rings:
+        some.step()
+    for copy in shares.values():
+        copy.wait_recv()
+    stores(1 - place.core)
     while any(some.flying for some in rings):
         for some in rings:
             some.step()

time: 155 us -> 153 us (0.987); the launches traced: 153 us -> 153 us
  no operation moved by 1% of the time
where the time goes in v5:
time: 153 us
  Pallas kernels  144 us (94%)
  local copies, waits for them, and re-layouts  8.02 us (5%)
    pallas_call x1, Pallas kernels, body(): pl.pallas_call(functools.partial(finish_kernel, zs), out_shape=(shape((to...  65.4 us
    pallas_call x1, Pallas kernels, body(): pl.pallas_call(functools.partial(keys_kernel, zs), out_shape=(shape((mode...  61.3 us
    pallas_call x1, Pallas kernels, body(): pl.pallas_call(functools.partial(attention_kernel, zs), out_shape=(jax.Sh...  17.8 us
    unnamed x19, local copies, waits for them, and re-layouts  8.02 us

profile of v5, /device:TPU:1, one launch (start us, length us, event | category | flops | bytes accessed | tf_op | source)
XLA Modules:
  0.0 153.2 jit_solution(13449509276081510145)
XLA Ops:
  0.6 0.0 copy-start.1
  0.6 1.2 copy-done.1
  1.9 0.0 copy-start.2
  1.9 0.9 copy-done.2
  2.8 0.0 copy-start.3
  2.8 0.9 copy-done.3
  3.7 0.0 copy-start.5
  3.7 0.7 copy-done.5
  4.4 0.0 copy-start.4
  4.4 0.0 copy-start.6
  4.4 61.3 %gather_weights_and_keys.1 = (bf16[8192,640]{1,0:T(8,128)(2,1)}, bf16[512,1024]{1,0:T(8,128)(2,1)S(1)}, bf16[512,1024]{1,0:T(8,128)(2,1)S(1)}, bf16[4096,128]{1,...) custom-call(bf16[1024,512]{1,0:T(8,128)(2,1)S(1)} %copy-done.1, ...), custom_call_target="tpu_custom_call" | custom-call | tf_op jit(solution)/shard_map/gather_weights_and_keys/pallas_call | solution.py:842
  65.7 0.0 copy-done.4
  65.7 0.0 copy-done.6
  65.8 0.0 copy-start
  65.8 17.8 %attention_gradients.1 = (bf16[512,1024]{1,0:T(8,128)(2,1)S(1)}, bf16[4096,256]{1,0:T(8,128)(2,1)S(1)}) custom-call(s32[64]{0:T(128)S(1)} %bitcast.18, s32[1,4096]{1,0:T(1,128)S(1)} %copy-done.4, s32[1,4096]{1,0:T(1,128)S(1)} %copy-done.4, bf16[512,1024]{1,0:T(8,128)(2,1)S(1)} %get-tuple-element.19.queries, ...), custom_call_target="tpu_custom_call" | custom-call | tf_op jit(solution)/shard_map/attention_gradients/pallas_call | solution.py:879
  83.5 0.0 copy-done
  83.6 65.4 %sum_gradients.1 = (bf16[128,4096]{1,0:T(8,128)(2,1)S(1)}, bf16[128,512]{1,0:T(8,128)(2,1)S(1)}, bf16[128,8192]{1,0:T(8,128)(2,1)S(1)}, f32[64,1024]{1,0:T(8,128)S(1)}, f32[64,64]{1,0:T(8,128)S(1)}) custom-call(bf16[4096,256]{1,0:T(8,128)(2,1)S(1)} %get-tuple-element.23.dkv_ref, bf16[512,1024]{1,0:T(8,128)(2,1)S(1)} %get-tuple-element.24.dqg_ref, ...), custom_call_target="tpu_custom_call" | custom-call | tf_op jit(solution)/shard_map/sum_gradients/pallas_call | solution.py:918
  148.9 1.0 copy.19
  149.9 0.7 copy.20
  150.6 1.3 copy.21
  151.9 0.7 copy.22
  152.6 0.6 copy.23
Async XLA Ops:
  0.6 1.2 copy-start.1
  1.9 0.9 copy-start.2
  2.8 0.9 copy-start.3
  3.7 0.7 copy-start.5
  4.4 61.4 %copy-start.4 = (s32[1,4096]{1,0:T(1,128)S(1)}, s32[1,4096]{1,0:T(1,128)}, u32[]{:S(2)}) copy-start(s32[1,4096]{1,0:T(1,128)} %doc_ref.1) | copy-start | bytes 49156
  4.4 61.4 %copy-start.6 = (s32[1,64]{1,0:T(1,128)S(1)}, s32[1,64]{1,0:T(1,128)}, u32[]{:S(2)}) copy-start(s32[1,64]{1,0:T(1,128)} %param.16) | copy-start | bytes 772
  65.8 17.8 %copy-start = (bf16[1,128,8192]{2,1,0:T(8,128)(2,1)S(1)}, bf16[1,128,8192]{2,1,0:T(8,128)(2,1)}, u32[]{:S(2)}) copy-start(bf16[1,128,8192]{2,1,0:T(8,128)(2,1)} %param.9) | copy-start | bytes 6291460
